TPU v7x, 128 devices: a whole 4x4x4 slice. The times are simulated.
128 devices in a mesh: seq: 64 (over x_lo, z, y, core), col: 2 (over x_hi).
Axes of the slice: x: 4 (x_hi: 2, x_lo: 2; x = x_hi * 2 + x_lo), y: 4, z: 4, core: 2. Of those that a mesh axis runs over, the one named last changes fastest.
Arguments:
- tokens: bfloat16 [65536, 512], P('seq', 'col'), may hold values from -50 to 50
- cotangent: bfloat16 [65536, 512], P('seq', 'col'), may hold values from -6 to 6
- weight_in: bfloat16 [512, 4, 4, 128], P(None, None, 'col'), may hold values from -0.25 to 0.25
- weight_out: bfloat16 [4, 128, 512], P('col'), may hold values from -0.25 to 0.25
- history_ids: int32 [65536], replicated, may hold values from 0 to 31, never falling along the last dimension, each value on 1 to 4096 neighbouring positions
Outputs:
- out: bfloat16 [65536, 512], P('seq', 'col')
- grad_tokens: bfloat16 [65536, 512], P('seq', 'col')
- grad_weight_in: float32 [512, 4, 4, 128], P(None, None, 'col')
- grad_weight_out: float32 [4, 128, 512], P('col')
Inputs may be any that keep to these rules, and one draw needn't show every extreme that they name: history_ids never fall along the stream; every id occurs; each history holds 1 to 4096 tokens and one holds exactly 4096.
All inputs are finite; a program needn't handle non-finite values.
Results may differ from a plain program's by a relative error of at most 0.0092.
Values may be sent and summed in bfloat16 or wider, within the bound.
A program may use at most 192 MiB of HBM per device.

v0:
```python
import math

import jax
import jax.numpy as jnp
from jax import lax
from jax.sharding import PartitionSpec as P

MAXLEN = 4096


epsilon = 1e-05
head_floor = 1.0


def passed_along(block, axis, distance):
    devices = range(lax.axis_size(axis))
    route = [(i - distance, i) for i in devices if i - distance in devices]
    return lax.ppermute(block, axis, route)


def layer_norm(values, offset):
    center = values - jnp.mean(values, axis=-1, keepdims=True)
    inv_std = lax.rsqrt(jnp.mean(center * center, axis=-1, keepdims=True) + offset)
    return (center * inv_std, inv_std)


def silu_slope(inputs):
    gate_value = jax.nn.sigmoid(inputs)
    return gate_value * (1.0 + inputs * (1.0 - gate_value))


def norm_back(grad_in, normed, inv_std):
    return inv_std * (
        grad_in
        - jnp.mean(grad_in, axis=-1, keepdims=True)
        - normed * jnp.mean(grad_in * normed, axis=-1, keepdims=True)
    )


def shards(tokens, cotangent, weight_in, weight_out, history_ids):
    row_count = tokens.shape[0]
    col_width = tokens.shape[1]
    seq_count = lax.axis_size("seq")
    device_pos = lax.axis_index("seq")
    score_scale = weight_out.shape[1] ** (-0.5)
    reach_count = (MAXLEN - 2 + row_count) // row_count
    positions = jnp.arange(row_count, dtype=jnp.int32)

    def block_ids(offset):
        source = device_pos - offset
        valid = (source >= 0) & (source < seq_count)
        safe_pos = jnp.clip(source, 0, seq_count - 1)
        return (lax.dynamic_slice_in_dim(history_ids, safe_pos * row_count, row_count), valid)

    def attend_some(operands):
        query_rows, key_rows, value_rows, allowed = operands
        scores = score_scale * jnp.einsum(
            "ihe,jhe->hij", query_rows, key_rows, preferred_element_type=jnp.float32
        )
        weights_att = (jax.nn.silu(scores) * allowed[None]).astype(jnp.bfloat16)
        return jnp.einsum(
            "hij,jhe->ihe", weights_att, value_rows, preferred_element_type=jnp.float32
        )

    def attend_skip(operands):
        return jnp.zeros(operands[0].shape, jnp.float32)

    def back_some(operands):
        query_rows, key_rows, value_rows, grad_rows, allowed = operands
        scores = score_scale * jnp.einsum(
            "ihe,jhe->hij", query_rows, key_rows, preferred_element_type=jnp.float32
        )
        weights_att = (jax.nn.silu(scores) * allowed[None]).astype(jnp.bfloat16)
        grad_att = jnp.einsum(
            "ihe,jhe->hij", grad_rows, value_rows, preferred_element_type=jnp.float32
        )
        grad_scores = (score_scale * allowed[None] * silu_slope(scores) * grad_att).astype(
            jnp.bfloat16
        )
        grad_query = jnp.einsum(
            "hij,jhe->ihe", grad_scores, key_rows, preferred_element_type=jnp.float32
        )
        grad_key = jnp.einsum(
            "hij,ihe->jhe", grad_scores, query_rows, preferred_element_type=jnp.float32
        )
        grad_value = jnp.einsum(
            "hij,ihe->jhe", weights_att, grad_rows, preferred_element_type=jnp.float32
        )
        return (grad_query, grad_key, grad_value)

    def back_skip(operands):
        return (
            jnp.zeros(operands[0].shape, jnp.float32),
            jnp.zeros(operands[1].shape, jnp.float32),
            jnp.zeros(operands[1].shape, jnp.float32),
        )

    gathered = (
        lax.all_gather(tokens, "col", axis=1, tiled=True),
        lax.all_gather(cotangent, "col", axis=1, tiled=True),
    )
    features = gathered[0].astype(jnp.float32)
    grad_full = gathered[1]
    normed, inv_std = layer_norm(features, epsilon)
    normed_b = normed.astype(jnp.bfloat16)
    pre_act = jnp.einsum("td,dphe->tphe", normed_b, weight_in, preferred_element_type=jnp.float32)
    project = jax.nn.silu(pre_act).astype(jnp.bfloat16)
    up_part = project[:, 0]
    value_part = project[:, 1]
    query_part = project[:, 2]
    key_part = project[:, 3]
    own_ids, own_valid = block_ids(0)
    own_mask = (
        (own_ids[:, None] == own_ids[None, :]) & (positions[None, :] <= positions[:, None])
    ).astype(jnp.float32)
    attended = attend_some((query_part, key_part, value_part, own_mask))
    remote = []
    for shift_by in range(1, reach_count + 1):
        key_far, value_far = passed_along((key_part, value_part), "seq", shift_by)
        ids_far, valid = block_ids(shift_by)
        far_mask = ((own_ids[:, None] == ids_far[None, :]) & valid).astype(jnp.float32)
        active = valid & (ids_far[row_count - 1] == own_ids[0])
        attended = attended + lax.cond(
            active, attend_some, attend_skip, (query_part, key_far, value_far, far_mask)
        )
        remote.append((key_far, value_far, far_mask, active))
    head_normed, head_scale = layer_norm(attended, head_floor)
    gated = (head_normed * up_part.astype(jnp.float32)).astype(jnp.bfloat16)
    out_part = jnp.einsum("the,hed->td", gated, weight_out, preferred_element_type=jnp.float32)
    grad_gated = jnp.einsum(
        "td,hed->the", grad_full, weight_out, preferred_element_type=jnp.float32
    )
    grad_up = grad_gated * head_normed
    grad_heads = norm_back(grad_gated * up_part.astype(jnp.float32), head_normed, head_scale)
    grad_narrow = grad_heads.astype(jnp.bfloat16)
    grad_query, grad_key, grad_value = back_some(
        (query_part, key_part, value_part, grad_narrow, own_mask)
    )
    for shift_by in range(1, reach_count + 1):
        key_far, value_far, far_mask, active = remote[shift_by - 1]
        far_grads = lax.cond(
            active, back_some, back_skip, (query_part, key_far, value_far, grad_narrow, far_mask)
        )
        grad_query = grad_query + far_grads[0]
        returned = (
            passed_along(far_grads[1].astype(jnp.bfloat16), "seq", -shift_by).astype(jnp.float32),
            passed_along(far_grads[2].astype(jnp.bfloat16), "seq", -shift_by).astype(jnp.float32),
        )
        grad_key = grad_key + returned[0]
        grad_value = grad_value + returned[1]
    grad_proj = jnp.stack([grad_up, grad_value, grad_query, grad_key], axis=1)
    grad_pre = (grad_proj * silu_slope(pre_act)).astype(jnp.bfloat16)
    grad_w_in = jnp.einsum("td,tphe->dphe", normed_b, grad_pre, preferred_element_type=jnp.float32)
    grad_w_out = jnp.einsum("the,td->hed", gated, grad_full, preferred_element_type=jnp.float32)
    grad_part = jnp.einsum("tphe,dphe->td", grad_pre, weight_in, preferred_element_type=jnp.float32)
    summed = lax.psum((grad_w_in, grad_w_out), "seq")
    inv_root = 1.0 / math.sqrt(row_count * seq_count)
    col_start = lax.axis_index("col") * col_width
    grad_own = cotangent.astype(jnp.float32)
    token_own = tokens.astype(jnp.float32)
    out = (
        token_own
        + lax.psum_scatter(
            out_part.astype(jnp.bfloat16), "col", scatter_dimension=1, tiled=True
        ).astype(jnp.float32)
    ).astype(jnp.bfloat16)
    grad_normed = lax.psum(grad_part.astype(jnp.bfloat16), "col").astype(jnp.float32)
    grad_whole = norm_back(grad_normed, normed, inv_std)
    grad_tokens = (lax.dynamic_slice_in_dim(grad_whole, col_start, col_width, 1) + grad_own).astype(
        jnp.bfloat16
    )
    return (out, grad_tokens, summed[0] * inv_root, summed[1] * inv_root)


def solution(mesh):
    placed = (
        P("seq", "col"),
        P("seq", "col"),
        P(None, None, "col", None),
        P("col", None, None),
        P(),
    )
    return jax.shard_map(
        shards,
        mesh=mesh,
        in_specs=placed,
        out_specs=(
            P("seq", "col"),
            P("seq", "col"),
            P(None, None, "col", None),
            P("col", None, None),
        ),
        check_vma=False,
    )
```

profile of v0, /device:TPU:1, one launch (start us, length us, event | category | flops | bytes accessed | tf_op | source)
XLA Modules:
  0.0 1025.2 jit_solution(7719497326622252241)
XLA Ops:
  12.1 26.1 %all-gather.3.cloned.1.call-done = bf16[1024,512]{1,0:T(8,128)(2,1)} async-done(((bf16[1024,256]{1,0:T(8,128)(2,1)}), bf16[1024,512]{1,0:T(8,128)(2,1)}) %all-gather.3.cloned.1.call-update) | async-done | bytes 1048592 | tf_op jit(solution)/shard_map/all_gather | solution.py:99
  46.4 6.0 collective-permute-start.5
  52.4 3.2 collective-permute-start.7
  55.5 3.9 collective-permute-start.6
  59.4 7.7 and_convert_fusion.3
  77.9 3.0 collective-permute-start.3
  82.9 5.0 collective-permute-start.4
  87.9 3.1 collective-permute-start.2
  93.0 5.4 multiply_convert_fusion.37
  102.2 16.2 %collective-permute-done.4 = bf16[1024,2,128]{0,2,1:T(8,128)(2,1)} collective-permute-done((bf16[1024,2,128]{0,2,1:T(8,128)(2,1)}, bf16[1024,2,128]{0,2,1:T(8,128)(2,1)}, u32[]{:S(2)}, u32[]{:S(2)}) %collective-permute-start.4) | collective-permute-done | bytes 524320 | tf_op jit(solution)/shard_map/ppermute | solution.py:18
  119.5 4.5 collective-permute-done.2
  125.1 4.5 collective-permute-done
  129.6 19.8 %conditional.8 = (f32[1024,2,128]{0,2,1:T(8,128)}) conditional(s32[]{:T(128)} %convert_element_type.182, () %tuple.64, (bf16[1024,2,128]{0,2,1:T(8,128)(2,1)S(1)}, bf16[1024,2,128]{0,2,1:T(8,128)(2,1)}, f32[1024,1024]{1,0:T(8,128)}, bf16[1024,2,128]{0,2,1:T(8,128)(2,1)}) %tuple.65), branch_computations={%region_2.3_spmd, %region_3.4_spmd} | conditional | flops 1088421888 | bytes 8912904 | solution.py:123
  139.8 7.1 fusion.3
  149.4 3.1 fusion.70
  158.7 23.2 %conditional.12 = (bf16[1024,2,128]{2,0,1:T(8,128)(2,1)}, bf16[1024,2,128]{2,0,1:T(8,128)(2,1)}, f32[1024,2,128]{0,2,1:T(8,128)}) conditional(s32[]{:T(128)} %convert_element_type.182, () %tuple.72, (f32[1024,1024]{1,0:T(8,128)S(1)}, bf16[1024,2,128]{0,2,1:T(8,128)(2,1)S(1)}, bf16[1024,2,128]{0,2,1:T(8,128)(2,1)}, ...), branch_computations={%region_15.16_spmd, %region_16.17_spmd} | conditional | flops 2723151872 | bytes 62390296 | solution.py:141
  163.6 4.3 fusion.25
  167.9 5.7 multiply_convert_fusion.17
  176.1 3.3 convolution_bitcast_fusion.1
  189.0 4.7 conditional.14
  195.7 4.6 conditional.15
  208.4 6.8 multiply_convert_fusion.36
  223.7 4.1 add_bitcast_fusion.1
  239.2 7.5 collective-permute-done.12
  249.5 15.1 %collective-permute-done.8 = bf16[1024,2,128]{0,2,1:T(8,128)(2,1)} collective-permute-done((bf16[1024,2,128]{0,2,1:T(8,128)(2,1)}, bf16[1024,2,128]{0,2,1:T(8,128)(2,1)}, u32[]{:S(2)}, u32[]{:S(2)}) %collective-permute-start.8) | collective-permute-done | bytes 524320 | tf_op jit(solution)/shard_map/ppermute | solution.py:18
  264.6 11.1 %collective-permute-done.9 = bf16[1024,2,128]{0,2,1:T(8,128)(2,1)S(1)} collective-permute-done((bf16[1024,2,128]{0,2,1:T(8,128)(2,1)}, bf16[1024,2,128]{0,2,1:T(8,128)(2,1)S(1)}, u32[]{:S(2)}, u32[]{:S(2)}) %collective-permute-start.9) | collective-permute-done | bytes 524320 | tf_op jit(solution)/shard_map/ppermute | solution.py:18
  275.7 28.1 %collective-permute-done.10 = bf16[1024,2,128]{0,2,1:T(8,128)(2,1)S(1)} collective-permute-done((bf16[1024,2,128]{0,2,1:T(8,128)(2,1)S(1)}, bf16[1024,2,128]{0,2,1:T(8,128)(2,1)S(1)}, u32[]{:S(2)}, u32[]{:S(2)}) %collective-permute-start.10) | collective-permute-done | bytes 524320 | tf_op jit(solution)/shard_map/ppermute | solution.py:18
  303.8 10.3 %collective-permute-done.11 = bf16[1024,2,128]{0,2,1:T(8,128)(2,1)S(1)} collective-permute-done((bf16[1024,2,128]{0,2,1:T(8,128)(2,1)}, bf16[1024,2,128]{0,2,1:T(8,128)(2,1)S(1)}, u32[]{:S(2)}, u32[]{:S(2)}) %collective-permute-start.11) | collective-permute-done | bytes 524320 | tf_op jit(solution)/shard_map/ppermute | solution.py:18
  323.9 4.6 fusion.56
  328.5 100.8 %all-reduce.4.cloned.1.call-done = bf16[1024,512]{1,0:T(8,128)(2,1)} async-done(((bf16[1024,512]{1,0:T(8,128)(2,1)}), bf16[1024,512]{1,0:T(8,128)(2,1)}) %all-reduce.4.cloned.1.call-update) | async-done | bytes 1048592 | tf_op jit(solution)/shard_map/psum | solution.py:167
  434.6 20.9 %reduce-scatter.2.cloned.1.call-done = bf16[1024,256]{1,0:T(8,128)(2,1)} async-done(((bf16[1024,512]{1,0:T(8,128)(2,1)}), bf16[1024,256]{1,0:T(8,128)(2,1)}) %reduce-scatter.2.cloned.1.call-update) | async-done | bytes 524304 | tf_op jit(solution)/shard_map/reduce_scatter | solution.py:163
  457.5 555.3 %all-reduce.6.cloned.1.call-done = (f32[512,4,2,128]{3,0,2,1:T(8,128)}, f32[2,128,512]{2,1,0:T(8,128)}) async-done(((f32[512,4,2,128]{3,0,2,1:T(8,128)}, f32[2,128,512]{2,1,0:T(8,128)}), (f32[512,4,2,128]{3,0,2,1:T(8,128)}, f32[2,128,512]{2,1,0:T(8,128)})) %all-reduce.6.cloned.1.call-update) | async-done | bytes 2621456 | tf_op jit(solution)/shard_map/psum | solution.py:156
  (145 shorter events, 120.1 us)
Async XLA Ops:
  7.2 146.5 %copy-start = (bf16[2,128,512]{2,1,0:T(8,128)(2,1)S(1)}, bf16[2,128,512]{2,1,0:T(8,128)(2,1)}, u32[]{:S(2)}) copy-start(bf16[2,128,512]{2,1,0:T(8,128)(2,1)} %param.24) | copy-start | bytes 786436
  7.2 31.0 %all-gather.3.cloned.1.call-start = ((), (), s32[]{:S(2)}) async-start(), calls=%async_computation.1 | async-start | bytes 1572864 | tf_op jit(solution)/shard_map/all_gather | solution.py:99
  7.9 145.7 %all-gather.5.cloned.1.call-start = ((), (), s32[]{:S(2)}) async-start(), calls=%async_computation.3 | async-start | bytes 1572864 | tf_op jit(solution)/shard_map/all_gather | solution.py:100
  8.7 420.7 %all-reduce.4.cloned.1.call-start = ((), (), s32[]{:S(2)}) async-start(), calls=%async_computation.4 | async-start | bytes 2097152 | tf_op jit(solution)/shard_map/psum | solution.py:167
  46.4 36.5 %collective-permute-start.5 = (bf16[1024,2,128]{0,2,1:T(8,128)(2,1)}, bf16[1024,2,128]{0,2,1:T(8,128)(2,1)}, u32[]{:S(2)}, u32[]{:S(2)}) collective-permute-start(bf16[1024,2,128]{0,2,1:T(8,128)(2,1)} %get-tuple-element.207), channel_id=1, source_target_pairs={{0,6},{2,8},{4,10},{6,12},{8,14},{10,16},{12,18},{14,20},{16,22},{... | collective-permute-start | bytes 1572872 | tf_op jit(solution)/shard_map/ppermute | solution.py:18
  52.4 35.5 %collective-permute-start.7 = (bf16[1024,2,128]{0,2,1:T(8,128)(2,1)}, bf16[1024,2,128]{0,2,1:T(8,128)(2,1)}, u32[]{:S(2)}, u32[]{:S(2)}) collective-permute-start(bf16[1024,2,128]{0,2,1:T(8,128)(2,1)} %get-tuple-element.207), channel_id=1, source_target_pairs={{0,8},{2,10},{4,12},{6,14},{8,16},{10,18},{12,20},{14,22},{16,24},... | collective-permute-start | bytes 1572872 | tf_op jit(solution)/shard_map/ppermute | solution.py:18
  55.5 35.5 %collective-permute-start.6 = (bf16[1024,2,128]{0,2,1:T(8,128)(2,1)}, bf16[1024,2,128]{0,2,1:T(8,128)(2,1)S(1)}, u32[]{:S(2)}, u32[]{:S(2)}) collective-permute-start(bf16[1024,2,128]{0,2,1:T(8,128)(2,1)} %get-tuple-element.208), channel_id=1, source_target_pairs={{0,8},{2,10},{4,12},{6,14},{8,16},{10,18},{12,20},{14,22},{16,24},... | collective-permute-start | bytes 1572872 | tf_op jit(solution)/shard_map/ppermute | solution.py:18
  75.2 17.8 %copy-start.16 = (f32[1024,1024]{1,0:T(8,128)S(1)}, f32[1024,1024]{1,0:T(8,128)}, u32[]{:S(2)}) copy-start(f32[1024,1024]{1,0:T(8,128)} %get-tuple-element.220) | copy-start | bytes 12582916
  77.9 41.6 %collective-permute-start.3 = (bf16[1024,2,128]{0,2,1:T(8,128)(2,1)}, bf16[1024,2,128]{0,2,1:T(8,128)(2,1)}, u32[]{:S(2)}, u32[]{:S(2)}) collective-permute-start(bf16[1024,2,128]{0,2,1:T(8,128)(2,1)} %get-tuple-element.207), channel_id=1, source_target_pairs={{0,4},{2,6},{4,8},{6,10},{8,12},{10,14},{12,16},{14,18},{16,20},{1... | collective-permute-start | bytes 1572872 | tf_op jit(solution)/shard_map/ppermute | solution.py:18
  81.0 44.1 %collective-permute-start.1 = (bf16[1024,2,128]{0,2,1:T(8,128)(2,1)}, bf16[1024,2,128]{0,2,1:T(8,128)(2,1)}, u32[]{:S(2)}, u32[]{:S(2)}) collective-permute-start(bf16[1024,2,128]{0,2,1:T(8,128)(2,1)} %get-tuple-element.207), channel_id=1, source_target_pairs={{0,2},{2,4},{4,6},{6,8},{8,10},{10,12},{12,14},{14,16},{16,18},{18... | collective-permute-start | bytes 1572872 | tf_op jit(solution)/shard_map/ppermute | solution.py:18
  82.9 35.5 %collective-permute-start.4 = (bf16[1024,2,128]{0,2,1:T(8,128)(2,1)}, bf16[1024,2,128]{0,2,1:T(8,128)(2,1)}, u32[]{:S(2)}, u32[]{:S(2)}) collective-permute-start(bf16[1024,2,128]{0,2,1:T(8,128)(2,1)} %get-tuple-element.208), channel_id=1, source_target_pairs={{0,6},{2,8},{4,10},{6,12},{8,14},{10,16},{12,18},{14,20},{16,22},{... | collective-permute-start | bytes 1572872 | tf_op jit(solution)/shard_map/ppermute | solution.py:18
  87.9 36.1 %collective-permute-start.2 = (bf16[1024,2,128]{0,2,1:T(8,128)(2,1)}, bf16[1024,2,128]{0,2,1:T(8,128)(2,1)}, u32[]{:S(2)}, u32[]{:S(2)}) collective-permute-start(bf16[1024,2,128]{0,2,1:T(8,128)(2,1)} %get-tuple-element.208), channel_id=1, source_target_pairs={{0,4},{2,6},{4,8},{6,10},{8,12},{10,14},{12,16},{14,18},{16,20},{1... | collective-permute-start | bytes 1572872 | tf_op jit(solution)/shard_map/ppermute | solution.py:18
  91.0 9.8 copy-start.21
  91.0 38.6 %collective-permute-start = (bf16[1024,2,128]{0,2,1:T(8,128)(2,1)}, bf16[1024,2,128]{0,2,1:T(8,128)(2,1)}, u32[]{:S(2)}, u32[]{:S(2)}) collective-permute-start(bf16[1024,2,128]{0,2,1:T(8,128)(2,1)} %get-tuple-element.208), channel_id=1, source_target_pairs={{0,2},{2,4},{4,6},{6,8},{8,10},{10,12},{12,14},{14,16},{16,18},{18... | collective-permute-start | bytes 1572872 | tf_op jit(solution)/shard_map/ppermute | solution.py:18
  153.6 5.1 copy-start.9
  202.4 29.7 %collective-permute-start.15 = (bf16[1024,2,128]{0,2,1:T(8,128)(2,1)}, bf16[1024,2,128]{0,2,1:T(8,128)(2,1)}, u32[]{:S(2)}, u32[]{:S(2)}) collective-permute-start(bf16[1024,2,128]{0,2,1:T(8,128)(2,1)} %copy.66), channel_id=1, source_target_pairs={{8,0},{10,2},{12,4},{14,6},{16,8},{18,10},{20,12},{22,14},{24,16},... | collective-permute-start | bytes 1572872 | tf_op jit(solution)/shard_map/ppermute | solution.py:18
  203.7 30.0 %collective-permute-start.14 = (bf16[1024,2,128]{0,2,1:T(8,128)(2,1)}, bf16[1024,2,128]{0,2,1:T(8,128)(2,1)}, u32[]{:S(2)}, u32[]{:S(2)}) collective-permute-start(bf16[1024,2,128]{0,2,1:T(8,128)(2,1)} %copy.65), channel_id=1, source_target_pairs={{6,0},{8,2},{10,4},{12,6},{14,8},{16,10},{18,12},{20,14},{22,16},{... | collective-permute-start | bytes 1572872 | tf_op jit(solution)/shard_map/ppermute | solution.py:18
  205.0 30.0 %collective-permute-start.13 = (bf16[1024,2,128]{0,2,1:T(8,128)(2,1)}, bf16[1024,2,128]{0,2,1:T(8,128)(2,1)}, u32[]{:S(2)}, u32[]{:S(2)}) collective-permute-start(bf16[1024,2,128]{0,2,1:T(8,128)(2,1)} %copy.64), channel_id=1, source_target_pairs={{4,0},{6,2},{8,4},{10,6},{12,8},{14,10},{16,12},{18,14},{20,16},{2... | collective-permute-start | bytes 1572872 | tf_op jit(solution)/shard_map/ppermute | solution.py:18
  206.3 40.5 %collective-permute-start.12 = (bf16[1024,2,128]{0,2,1:T(8,128)(2,1)}, bf16[1024,2,128]{0,2,1:T(8,128)(2,1)}, u32[]{:S(2)}, u32[]{:S(2)}) collective-permute-start(bf16[1024,2,128]{0,2,1:T(8,128)(2,1)} %copy.63), channel_id=1, source_target_pairs={{2,0},{4,2},{6,4},{8,6},{10,8},{12,10},{14,12},{16,14},{18,16},{20... | collective-permute-start | bytes 1572872 | tf_op jit(solution)/shard_map/ppermute | solution.py:18
  221.8 42.8 %collective-permute-start.8 = (bf16[1024,2,128]{0,2,1:T(8,128)(2,1)}, bf16[1024,2,128]{0,2,1:T(8,128)(2,1)}, u32[]{:S(2)}, u32[]{:S(2)}) collective-permute-start(bf16[1024,2,128]{0,2,1:T(8,128)(2,1)} %copy.41), channel_id=1, source_target_pairs={{2,0},{4,2},{6,4},{8,6},{10,8},{12,10},{14,12},{16,14},{18,16},{20... | collective-permute-start | bytes 1572872 | tf_op jit(solution)/shard_map/ppermute | solution.py:18
  232.1 14.6 %copy-start.5 = (bf16[2,1024,1024]{2,1,0:T(8,128)(2,1)S(1)}, bf16[2,1024,1024]{2,1,0:T(8,128)(2,1)}, u32[]{:S(2)}) copy-start(bf16[2,1024,1024]{2,1,0:T(8,128)(2,1)} %copy-done.4) | copy-start | bytes 12582916
  232.1 43.6 %collective-permute-start.9 = (bf16[1024,2,128]{0,2,1:T(8,128)(2,1)}, bf16[1024,2,128]{0,2,1:T(8,128)(2,1)S(1)}, u32[]{:S(2)}, u32[]{:S(2)}) collective-permute-start(bf16[1024,2,128]{0,2,1:T(8,128)(2,1)} %copy.46), channel_id=1, source_target_pairs={{4,0},{6,2},{8,4},{10,6},{12,8},{14,10},{16,12},{18,14},{20,16},{2... | collective-permute-start | bytes 1572872 | tf_op jit(solution)/shard_map/ppermute | solution.py:18
  233.7 70.1 %collective-permute-start.10 = (bf16[1024,2,128]{0,2,1:T(8,128)(2,1)S(1)}, bf16[1024,2,128]{0,2,1:T(8,128)(2,1)S(1)}, u32[]{:S(2)}, u32[]{:S(2)}) collective-permute-start(bf16[1024,2,128]{0,2,1:T(8,128)(2,1)S(1)} %copy.51), channel_id=1, source_target_pairs={{6,0},{8,2},{10,4},{12,6},{14,8},{16,10},{18,12},{20,14},{22,16},{... | collective-permute-start | bytes 1572872 | tf_op jit(solution)/shard_map/ppermute | solution.py:18
  235.0 79.1 %collective-permute-start.11 = (bf16[1024,2,128]{0,2,1:T(8,128)(2,1)}, bf16[1024,2,128]{0,2,1:T(8,128)(2,1)S(1)}, u32[]{:S(2)}, u32[]{:S(2)}) collective-permute-start(bf16[1024,2,128]{0,2,1:T(8,128)(2,1)} %copy.56), channel_id=1, source_target_pairs={{8,0},{10,2},{12,4},{14,6},{16,8},{18,10},{20,12},{22,14},{24,16},... | collective-permute-start | bytes 1572872 | tf_op jit(solution)/shard_map/ppermute | solution.py:18
  239.2 76.4 %copy-start.3 = (f32[1024,1024]{0,1:S(1)}, f32[1024,1024]{0,1}, u32[]{:S(2)}) copy-start(f32[1024,1024]{0,1} %copy-done.2) | copy-start | bytes 12582916
  239.2 76.4 %copy-start.13 = (f32[1024,1,2,128]{0,3,2,1:T(8,128)S(1)}, f32[1024,1,2,128]{0,3,2,1:T(8,128)}, u32[]{:S(2)}) copy-start(f32[1024,1,2,128]{0,3,2,1:T(8,128)} %get-tuple-element.206) | copy-start | bytes 3145732
  239.2 76.4 %copy-start.14 = (f32[1024,1,2,128]{0,3,2,1:T(8,128)S(1)}, f32[1024,1,2,128]{0,3,2,1:T(8,128)}, u32[]{:S(2)}) copy-start(f32[1024,1,2,128]{0,3,2,1:T(8,128)} %add_bitcast_fusion.1) | copy-start | bytes 3145732
  320.8 134.7 %reduce-scatter.2.cloned.1.call-start = ((), (), s32[]{:S(2)}) async-start(), calls=%async_computation.2 | async-start | bytes 1572864 | tf_op jit(solution)/shard_map/reduce_scatter | solution.py:163
  322.4 690.4 %all-reduce.6.cloned.1.call-start = ((), (), s32[]{:S(2)}) async-start(), calls=%async_computation.5 | async-start | bytes 5242880 | tf_op jit(solution)/shard_map/psum | solution.py:156
  328.5 104.8 %copy-start.20 = (bf16[1024,256]{1,0:T(8,128)(2,1)S(1)}, bf16[1024,256]{1,0:T(8,128)(2,1)}, u32[]{:S(2)}) copy-start(bf16[1024,256]{1,0:T(8,128)(2,1)} %param.22) | copy-start | bytes 1572868
  430.9 24.6 %copy-start.18 = (bf16[1024,256]{1,0:T(8,128)(2,1)S(1)}, bf16[1024,256]{1,0:T(8,128)(2,1)}, u32[]{:S(2)}) copy-start(bf16[1024,256]{1,0:T(8,128)(2,1)} %param.21) | copy-start | bytes 1572868
  1012.8 4.8 copy-start.25
  (13 other events, 32.7 us)
Sparse Core Ops, SparseCore 0:
  9.7 28.4 all-gather.2
  39.8 24.7 all-gather.4
  320.9 108.3 all-reduce.3
  431.7 23.7 reduce-scatter.1
  458.5 554.2 all-reduce.5
where the time goes:
time: 1030 us
  waiting for transfers between devices  802 us (78%)
  matrix products  62.4 us (6%)
  local copies, waits for them, and re-layouts  45.1 us (4%)
  starting transfers between devices  40.5 us (4%)
  other arithmetic  40.3 us (4%)
  between operations  19.7 us (2%)
  loops' own time  15.1 us (1%)
    psum x1, waiting for transfers between devices, shards(): summed = lax.psum((grad_w_in, grad_w_out), 'seq')  555 us
    psum x1, waiting for transfers between devices, shards(): lax.psum(grad_part.astype(jnp.bfloat16), 'col').astype(jnp.float32)  101 us
    ppermute x16, waiting for transfers between devices, passed_along(): return lax.ppermute(block, axis, route)  97.4 us
    ppermute x16, starting transfers between devices, passed_along(): return lax.ppermute(block, axis, route)  40 us
    all_gather x1, waiting for transfers between devices, shards(): lax.all_gather(tokens, 'col', axis=1, tiled=True)  26.1 us
    reduce_scatter x1, waiting for transfers between devices, shards(): lax.psum_scatter(out_part.astype(jnp.bfloat16), 'col', scatter_dimension=...  20.9 us
  transfers between devices with their start and end apart: 21, of which 12 were waited for; matrix products, arithmetic and copies ran while one was open for 9% of the time, Pallas kernels for 0%

commit v1 on v0

v1 whole, which is shorter than its diff:
```python
import functools
import math

import jax
import jax.numpy as jnp
from jax import lax
from jax.experimental import pallas as pl
from jax.experimental.pallas import tpu as pltpu
from jax.sharding import PartitionSpec as P

MESH = pl.DeviceIdType.MESH
F32 = jnp.float32
BF16 = jnp.bfloat16

T = 1024
R = 2 * T
D = 512
E = 128
HALF = D // 2
CH = 256
NCH = T // CH
TQ = 512
TK = 512
WIN = 3 * R
EPS = 1e-5
FLOOR = 1.0
SCALE = E**-0.5
OUT_OF_MASK = -32.0
GR = D + E
YR = GR // 4
XR = YR // 2

NT = (((1,), (1,)), ((), ()))
TN = (((0,), (0,)), ((), ()))


def dot(a, b, dims=(((1,), (0,)), ((), ()))):
    return lax.dot_general(a, b, dims, preferred_element_type=F32)


def place():
    s = lax.axis_index("seq")
    c = lax.axis_index("col")
    return s, c


def greet(partners):
    barrier = pltpu.get_barrier_semaphore()
    for partner in partners:
        pl.semaphore_signal(barrier, inc=1, device_id=partner, device_id_type=MESH)
    pl.semaphore_wait(barrier, len(partners))


def send(src, dst, send_sem, recv_sem, device):
    copy = pltpu.make_async_remote_copy(
        src_ref=src,
        dst_ref=dst,
        send_sem=send_sem,
        recv_sem=recv_sem,
        device_id=device,
        device_id_type=MESH,
    )
    copy.start()
    return copy


def rows_at(start, size):
    return pl.ds(pl.multiple_of(start, size), size)


def project_kernel(
    tok_ref, cot_ref, w_ref, nb_ref, rs_ref, q_ref, up_ref, kv_ref, cg_ref, xg, ss, rs, kss, krs
):
    s, c = place()
    core = lax.rem(s, 2)
    other = (s + 1 - 2 * core, c)
    far = (s, 1 - c)
    n = lax.axis_size("seq")
    ahead = [(lax.rem(s + 2 * k, n), c) for k in (1, 2)]
    behind = [(lax.rem(s + n - 2 * k, n), c) for k in (1, 2)]
    greet([other, far] + ahead + behind)

    base = core * T
    obase = (1 - core) * T

    copies = []
    x_copies = {}
    for kind, (src, buf) in enumerate(((tok_ref, xg), (cot_ref, cg_ref))):
        for i in range(NCH):
            dst = buf.at[c, rows_at(base + i * CH, CH)]
            x_copies[kind, i] = send(
                src.at[pl.ds(i * CH, CH)], dst, ss.at[kind, 0, i], rs.at[kind, 0, i], far
            )
    o_copies = {}
    for kind, (src, buf) in enumerate(((tok_ref, xg), (cot_ref, cg_ref))):
        for i in range(NCH):
            dst = buf.at[c, rows_at(base + i * CH, CH)]
            o_copies[kind, i] = send(
                src.at[pl.ds(i * CH, CH)], dst, ss.at[kind, 1, i], rs.at[kind, 1, i], other
            )
    for i in range(NCH):
        xg[c, rows_at(base + i * CH, CH)] = tok_ref[pl.ds(i * CH, CH)]
        cg_ref[c, rows_at(base + i * CH, CH)] = cot_ref[pl.ds(i * CH, CH)]

    def forward(kind, i):
        buf = (xg, cg_ref)[kind]
        x_copies[kind, i].wait_recv()
        where = buf.at[1 - c, rows_at(base + i * CH, CH)]
        return send(where, where, ss.at[kind, 2, i], rs.at[kind, 2, i], other)

    def compute(start, slot):
        rr = rows_at(start, CH)
        x0 = xg[0, rr].astype(F32)
        x1 = xg[1, rr].astype(F32)
        mean = (jnp.sum(x0, -1, keepdims=True) + jnp.sum(x1, -1, keepdims=True)) * (1.0 / D)
        x0 = x0 - mean
        x1 = x1 - mean
        var = (
            jnp.sum(x0 * x0, -1, keepdims=True) + jnp.sum(x1 * x1, -1, keepdims=True)
        ) * (1.0 / D)
        inv = lax.rsqrt(var + EPS)
        n0 = (x0 * inv).astype(BF16)
        n1 = (x1 * inv).astype(BF16)
        nb_ref[rr, :HALF] = n0
        nb_ref[rr, HALF:] = n1
        rs_ref[rr] = jnp.broadcast_to(inv, (CH, E))
        half = 0.5 * (dot(n0, w_ref[:HALF]) + dot(n1, w_ref[HALF:]))
        proj = (half + half * jnp.tanh(half)).astype(BF16)
        up_ref[rr] = proj[:, :E]
        q_ref[rr] = proj[:, 2 * E : 3 * E]
        kv_ref[2, rr, :E] = proj[:, 3 * E :]
        kv_ref[2, rr, E:] = proj[:, E : 2 * E]
        for k in (0, 1):
            copies.append(
                send(
                    kv_ref.at[2, rr],
                    kv_ref.at[1 - k, rr],
                    kss.at[k, slot],
                    krs.at[k, slot],
                    ahead[k],
                )
            )

    f_copies = {}
    for i in range(NCH):
        f_copies[0, i] = forward(0, i)
        compute(base + i * CH, i)
        o_copies[0, i].wait_recv()
        f_copies[0, i].wait_recv()
        compute(obase + i * CH, NCH + i)
    for i in range(NCH):
        f_copies[1, i] = forward(1, i)
    for i in range(NCH):
        o_copies[1, i].wait_recv()
        f_copies[1, i].wait_recv()
    for copy in list(x_copies.values()) + list(o_copies.values()) + list(f_copies.values()):
        copy.wait_send()
    for copy in copies:
        copy.wait()


def project(tokens, cotangent, w):
    vm = pl.BlockSpec(memory_space=pltpu.VMEM)
    return pl.pallas_call(
        project_kernel,
        out_shape=(
            jax.ShapeDtypeStruct((R, D), BF16),
            jax.ShapeDtypeStruct((R, E), F32),
            jax.ShapeDtypeStruct((R, E), BF16),
            jax.ShapeDtypeStruct((R, E), BF16),
            jax.ShapeDtypeStruct((3, R, 2 * E), BF16),
            jax.ShapeDtypeStruct((2, R, HALF), BF16),
        ),
        in_specs=[vm] * 3,
        out_specs=(vm,) * 6,
        scratch_shapes=[
            pltpu.VMEM((2, R, HALF), BF16),
            pltpu.SemaphoreType.DMA((2, 3, NCH)),
            pltpu.SemaphoreType.DMA((2, 3, NCH)),
            pltpu.SemaphoreType.DMA((2, 2 * NCH)),
            pltpu.SemaphoreType.DMA((2, 2 * NCH)),
        ],
        compiler_params=pltpu.CompilerParams(
            collective_id=0, has_side_effects=True, vmem_limit_bytes=56 * 1024 * 1024
        ),
        cost_estimate=pl.CostEstimate(flops=2 * R * D * D, bytes_accessed=16 << 20, transcendentals=R * D),
        name="gather_project",
    )(tokens, cotangent, w)


def attention_kernel(
    lo_ref, q_ref, kv_ref, up_ref, cg_ref, wo_ref, id_ref,
    op_ref, gated_ref, dup_ref, dq_ref, dkv_ref, dfar_ref,
    idc, acc,
):
    for j in range(WIN // E):
        row = id_ref[0:1, j * E : (j + 1) * E]
        idc[j * E : (j + 1) * E, :] = jnp.broadcast_to(row, (E, E)).T

    @pl.loop(0, WIN // TK)
    def _(j):
        acc[rows_at(j * TK, TK), :] = jnp.zeros((TK, 2 * E), F32)

    def spread(column, width):
        return jnp.concatenate([column] * (width // E), axis=1)

    first = 2 * R // TK

    @pl.loop(0, R // TQ)
    def _(t):
        rr = rows_at(t * TQ, TQ)
        q = q_ref[rr, :]
        wr = rows_at(2 * R + t * TQ, TQ)
        idq_col = idc[wr, :]
        idq_row = id_ref[0:1, wr]
        low = lo_ref[t]
        last = first + t * TQ // TK

        def forward(kt, total, causal):
            kr = rows_at(kt * TK, TK)
            half = dot(q, kv_ref[kr, :E], NT) * (0.5 * SCALE)
            ok = spread(idq_col, TK) == id_ref[0:1, kr]
            if causal:
                ri = lax.broadcasted_iota(jnp.int32, (TQ, TK), 0)
                ci = lax.broadcasted_iota(jnp.int32, (TQ, TK), 1)
                ok = ok & (ci <= ri)
            half = jnp.where(ok, half, OUT_OF_MASK)
            weights = (half + half * jnp.tanh(half)).astype(BF16)
            return total + dot(weights, kv_ref[kr, E:])

        att = lax.fori_loop(
            low, last, functools.partial(forward, causal=False), jnp.zeros((TQ, E), F32)
        )
        att = forward(last, att, True)

        center = att - jnp.mean(att, -1, keepdims=True)
        scale = lax.rsqrt(jnp.mean(center * center, -1, keepdims=True) + FLOOR)
        hn = center * scale
        up = up_ref[rr, :].astype(F32)
        gated = (hn * up).astype(BF16)
        gated_ref[rr, :] = gated
        op_ref[0, rr, :] = dot(gated, wo_ref[:, :HALF]).astype(BF16)
        op_ref[1, rr, :] = dot(gated, wo_ref[:, HALF:]).astype(BF16)
        gg = dot(cg_ref[0, rr, :], wo_ref[:, :HALF], NT) + dot(cg_ref[1, rr, :], wo_ref[:, HALF:], NT)
        dup_ref[rr, :] = gg * hn
        b = gg * up
        grad = (
            scale
            * (b - jnp.mean(b, -1, keepdims=True) - hn * jnp.mean(b * hn, -1, keepdims=True))
        ).astype(BF16)

        def backward(kt, total, causal):
            kr = rows_at(kt * TK, TK)
            k = kv_ref[kr, :E]
            half = dot(k, q, NT) * (0.5 * SCALE)
            ok = spread(idc[kr, :], TQ) == idq_row
            if causal:
                ri = lax.broadcasted_iota(jnp.int32, (TK, TQ), 0)
                ci = lax.broadcasted_iota(jnp.int32, (TK, TQ), 1)
                ok = ok & (ri <= ci)
            half = jnp.where(ok, half, OUT_OF_MASK)
            tan = jnp.tanh(half)
            weights = half + half * tan
            tan = 0.5 * tan
            slope = (0.5 + tan) + weights * (0.5 - tan)
            ds = (slope * dot(kv_ref[kr, E:], grad, NT)).astype(BF16)
            acc[kr, :E] += dot(ds, q)
            acc[kr, E:] += dot(weights.astype(BF16), grad)
            return total + dot(ds, k, TN)

        dq = lax.fori_loop(
            low, last, functools.partial(backward, causal=False), jnp.zeros((TQ, E), F32)
        )
        dq_ref[rr, :] = backward(last, dq, True) * SCALE

    @pl.loop(0, R // TK)
    def _(j):
        rr = rows_at(j * TK, TK)
        own = rows_at(2 * R + j * TK, TK)
        dkv_ref[rr, :E] = acc[own, :E] * SCALE
        dkv_ref[rr, E:] = acc[own, E:]
        for k in range(2):
            src = rows_at(k * R + j * TK, TK)
            dfar_ref[k, rr, :E] = (acc[src, :E] * SCALE).astype(BF16)
            dfar_ref[k, rr, E:] = acc[src, E:].astype(BF16)


def attention(lo, q, kv, up, cg, wo, ids):
    vm = pl.BlockSpec(memory_space=pltpu.VMEM)
    return pl.pallas_call(
        attention_kernel,
        out_shape=(
            jax.ShapeDtypeStruct((2, R, HALF), BF16),
            jax.ShapeDtypeStruct((R, E), BF16),
            jax.ShapeDtypeStruct((R, E), F32),
            jax.ShapeDtypeStruct((R, E), F32),
            jax.ShapeDtypeStruct((R, 2 * E), F32),
            jax.ShapeDtypeStruct((2, R, 2 * E), BF16),
        ),
        in_specs=[pl.BlockSpec(memory_space=pltpu.SMEM)] + [vm] * 6,
        out_specs=(vm,) * 6,
        scratch_shapes=[
            pltpu.VMEM((WIN, E), jnp.int32),
            pltpu.VMEM((WIN, 2 * E), F32),
        ],
        compiler_params=pltpu.CompilerParams(vmem_limit_bytes=56 * 1024 * 1024),
        cost_estimate=pl.CostEstimate(
            flops=7 * 2 * R * R * 2 * E, bytes_accessed=16 << 20, transcendentals=4 * R * R
        ),
        name="attention",
    )(lo, q, kv, up, cg, wo, ids)


SR = 512
NSR = R // SR
SC = 256
NSC = T // SC


def gradient_kernel(
    tok_ref, cot_ref, w_ref, nb_ref, rs_ref, cg_ref, gated_ref, op_ref, dup_ref, dq_ref, dkv_ref, dfar_ref,
    out_ref, gt_ref, gw_ref,
    back, slope, gp, part, chip_sum, to_col, from_col,
    gw, ybuf, yrecv, zacc, zbuf, zrecv, xacc, xbuf, xrecv, all_bf,
    bss, brs, sss, srs, ass, ars,
):
    s, c = place()
    n = lax.axis_size("seq")
    core = lax.rem(s, 2)
    y = lax.rem(lax.div(s, 2), 4)
    z = lax.rem(lax.div(s, 8), 4)
    xl = lax.div(s, 32)
    other = (s + 1 - 2 * core, c)
    far = (s, 1 - c)
    ahead = [(lax.rem(s + 2 * k, n), c) for k in (1, 2)]
    behind = [(lax.rem(s + n - 2 * k, n), c) for k in (1, 2)]
    ys = [lax.rem(y + k, 4) for k in (1, 2, 3)]
    zs = [lax.rem(z + k, 4) for k in (1, 2, 3)]
    yds = [(s + 2 * (v - y), c) for v in ys]
    zds = [(s + 8 * (v - z), c) for v in zs]
    xd = (s + 32 * (1 - 2 * xl), c)
    greet([other, far, xd] + ahead + behind + yds + zds)

    base = core * T
    obase = (1 - core) * T

    def to_core(kind, i):
        src = (op_ref, part)[kind].at[:, rows_at(obase + i * SC, SC)]
        dst = chip_sum.at[kind, :, pl.ds(i * SC, SC)]
        return send(src, dst, sss.at[kind, 0, i], srs.at[kind, 0, i], other)

    def across(kind, i, copy):
        copy.wait_recv()
        src = (op_ref, part)[kind]
        here = pl.ds(i * SC, SC)
        mine = src[1 - c, rows_at(base + i * SC, SC)].astype(F32)
        to_col[kind, here] = (mine + chip_sum[kind, 1 - c, here].astype(F32)).astype(BF16)
        return send(
            to_col.at[kind, here], from_col.at[kind, here], sss.at[kind, 1, i], srs.at[kind, 1, i], far
        )

    def finish(kind, i, copy):
        copy.wait_recv()
        here = pl.ds(i * SC, SC)
        src, own, out = ((op_ref, tok_ref, out_ref), (part, cot_ref, gt_ref))[kind]
        total = src[c, rows_at(base + i * SC, SC)].astype(F32)
        total = total + chip_sum[kind, c, here].astype(F32)
        total = total + from_col[kind, here].astype(F32)
        out[here] = (own[here].astype(F32) + total).astype(BF16)

    done = []
    out_core = [to_core(0, i) for i in range(NSC)]
    returned = []
    for i in range(NSR):
        rr = pl.ds(i * SR, SR)
        for k in (0, 1):
            returned.append(
                send(dfar_ref.at[1 - k, rr], back.at[k, rr], bss.at[k, i], brs.at[k, i], behind[k])
            )
    done += out_core + returned

    @pl.loop(0, R // SR)
    def _(i):
        rr = rows_at(i * SR, SR)
        half = 0.5 * dot(nb_ref[rr, :], w_ref[...])
        tan = jnp.tanh(half)
        silu = half + half * tan
        tan = 0.5 * tan
        sl = (0.5 + tan) + silu * (0.5 - tan)
        gp[rr, :E] = (dup_ref[rr, :] * sl[:, :E]).astype(BF16)
        gp[rr, 2 * E : 3 * E] = (dq_ref[rr, :] * sl[:, 2 * E : 3 * E]).astype(BF16)
        slope[rr, :E] = sl[:, 3 * E :]
        slope[rr, E:] = sl[:, E : 2 * E]

    out_far = [across(0, i, out_core[i]) for i in range(NSC)]
    done += out_far

    gw[D:, :HALF] = dot(gated_ref[...], cg_ref[0], TN)
    gw[D:, HALF:] = dot(gated_ref[...], cg_ref[1], TN)

    for i in range(NSR):
        rr = pl.ds(i * SR, SR)
        for k in (0, 1):
            returned[2 * i + k].wait_recv()
        g = dkv_ref[rr, :] + back[0, rr].astype(F32) + back[1, rr].astype(F32)
        g = (g * slope[rr, :]).astype(BF16)
        gp[rr, 3 * E :] = g[:, :E]
        gp[rr, E : 2 * E] = g[:, E:]

    for j in range(2):
        half = slice(j * HALF, (j + 1) * HALF)
        gw[:D, half] = dot(nb_ref[...], gp[:, half], TN)

    ybuf[...] = gw[...].astype(BF16)
    y_copies = [
        send(ybuf.at[rows_at(ys[k] * YR, YR)], yrecv.at[k], ass.at[0, k], ars.at[0, k], yds[k])
        for k in range(3)
    ]

    def tokens_back(i):
        rr = pl.ds(i * SR, SR)
        g = dot(gp[rr, :], w_ref[...], NT)
        nb = nb_ref[rr, :].astype(F32)
        inv = rs_ref[rr, 0:1]
        g = inv * (g - jnp.mean(g, -1, keepdims=True) - nb * jnp.mean(g * nb, -1, keepdims=True))
        part[0, rr] = g[:, :HALF].astype(BF16)
        part[1, rr] = g[:, HALF:].astype(BF16)

    for i in range(NSR):
        tokens_back(i)
    gt_core = [to_core(1, i) for i in range(NSC)]

    for copy in y_copies:
        copy.wait_recv()
    total = gw[rows_at(y * YR, YR), :]
    for k in range(3):
        total = total + yrecv[k].astype(F32)
    for j in range(4):
        zacc[j] = total[:, j * E : (j + 1) * E]
        zbuf[j] = total[:, j * E : (j + 1) * E].astype(BF16)
    z_copies = [
        send(zbuf.at[zs[k]], zrecv.at[k], ass.at[1, k], ars.at[1, k], zds[k]) for k in range(3)
    ]
    gt_far = [across(1, i, gt_core[i]) for i in range(NSC)]
    for copy in z_copies:
        copy.wait_recv()
    total = zacc[z]
    for k in range(3):
        total = total + zrecv[k].astype(F32)
    xacc[...] = total
    xbuf[...] = total.astype(BF16)
    x_copy = send(
        xbuf.at[rows_at((1 - xl) * XR, XR)], xrecv, ass.at[2, 0], ars.at[2, 0], xd
    )
    x_copy.wait_recv()
    mine = rows_at(xl * XR, XR)
    all_bf[core, y, z, mine] = (xacc[mine, :] + xrecv[...].astype(F32)).astype(BF16)
    done += y_copies + z_copies + [x_copy]

    spot = all_bf.at[core, y, z, mine]
    g_copy = send(spot, spot, ass.at[3, 0], ars.at[3, 0], xd)
    g_copy.wait_recv()
    spot = all_bf.at[core, y, z]
    gz = [send(spot, spot, ass.at[4, k], ars.at[4, k], zds[k]) for k in range(3)]
    for copy in gz:
        copy.wait_recv()
    spot = all_bf.at[core, y]
    gy = [send(spot, spot, ass.at[5, k], ars.at[5, k], yds[k]) for k in range(3)]
    gc = [send(spot, spot, ass.at[6, 0], ars.at[6, 0], other)]
    for k in range(3):
        gy[k].wait_recv()
        spot = all_bf.at[core, lax.rem(y + 3 - k, 4)]
        gc.append(send(spot, spot, ass.at[6, k + 1], ars.at[6, k + 1], other))
    done += [g_copy] + gz + gy + gc

    for i in range(NSC):
        finish(0, i, out_far[i])
    for i in range(NSC):
        finish(1, i, gt_far[i])
    done += gt_core + gt_far
    for copy in gc:
        copy.wait_recv()
    for h in range(2):
        for v in range(4):
            for j in range(4):
                gw_ref[h, v * YR : (v + 1) * YR, j * E : (j + 1) * E] = (
                    all_bf[h, v, j].astype(F32) * (1.0 / 256.0)
                )
    for copy in done:
        copy.wait_send()


def gradients(*operands):
    vm = pl.BlockSpec(memory_space=pltpu.VMEM)
    dma = pltpu.SemaphoreType.DMA
    return pl.pallas_call(
        gradient_kernel,
        out_shape=(
            jax.ShapeDtypeStruct((T, HALF), BF16),
            jax.ShapeDtypeStruct((T, HALF), BF16),
            jax.ShapeDtypeStruct((2, GR, D), F32),
        ),
        in_specs=[vm] * 12,
        out_specs=(vm,) * 3,
        scratch_shapes=[
            pltpu.VMEM((2, R, 2 * E), BF16),
            pltpu.VMEM((R, 2 * E), F32),
            pltpu.VMEM((R, 4 * E), BF16),
            pltpu.VMEM((2, R, HALF), BF16),
            pltpu.VMEM((2, 2, T, HALF), BF16),
            pltpu.VMEM((2, T, HALF), BF16),
            pltpu.VMEM((2, T, HALF), BF16),
            pltpu.VMEM((GR, D), F32),
            pltpu.VMEM((GR, D), BF16),
            pltpu.VMEM((3, YR, D), BF16),
            pltpu.VMEM((4, YR, E), F32),
            pltpu.VMEM((4, YR, E), BF16),
            pltpu.VMEM((3, YR, E), BF16),
            pltpu.VMEM((YR, E), F32),
            pltpu.VMEM((YR, E), BF16),
            pltpu.VMEM((XR, E), BF16),
            pltpu.VMEM((2, 4, 4, YR, E), BF16),
            dma((2, NSR)),
            dma((2, NSR)),
            dma((2, 2, NSC)),
            dma((2, 2, NSC)),
            dma((7, 4)),
            dma((7, 4)),
        ],
        compiler_params=pltpu.CompilerParams(
            collective_id=1, has_side_effects=True, vmem_limit_bytes=56 * 1024 * 1024
        ),
        cost_estimate=pl.CostEstimate(
            flops=7 * R * D * D, bytes_accessed=16 << 20, transcendentals=R * D
        ),
        name="gradients",
    )(*operands)


def shards(tokens, cotangent, weight_in, weight_out, history_ids):
    s = lax.axis_index("seq")
    core = s % 2
    chip = s // 2
    w = lax.dynamic_index_in_dim(weight_in, core, 2, keepdims=False).reshape(D, 4 * E)
    wo = lax.dynamic_index_in_dim(weight_out, core, 0, keepdims=False)
    padded = jnp.concatenate([jnp.full((2 * R,), -1, jnp.int32), history_ids])
    ids = lax.dynamic_slice_in_dim(padded, chip * R, WIN)
    firsts = lax.slice_in_dim(ids, 2 * R, WIN, TQ)
    lo = jnp.sum((ids[None, :] < firsts[:, None]).astype(jnp.int32), axis=1) // TK

    nb, inv, q, up, kv, cg = project(tokens, cotangent, w)
    op, gated, dup, dq, dkv, dfar = attention(
        lo, q, kv.reshape(WIN, 2 * E), up, cg, wo, ids.reshape(1, WIN)
    )
    out, gt, gw = gradients(
        tokens, cotangent, w, nb, inv, cg, gated, op, dup, dq, dkv, dfar
    )
    gwi = gw[:, :D].reshape(2, D, 4, E).transpose(1, 2, 0, 3)
    return out, gt, gwi, gw[:, D:]


def solution(mesh):
    placed = (
        P("seq", "col"),
        P("seq", "col"),
        P(None, None, "col", None),
        P("col", None, None),
        P(),
    )
    return jax.shard_map(
        shards,
        mesh=mesh,
        in_specs=placed,
        out_specs=(
            P("seq", "col"),
            P("seq", "col"),
            P(None, None, "col", None),
            P("col", None, None),
        ),
        check_vma=False,
    )
```

time: 1030 us -> 270 us (0.26)
  waiting for transfers between devices: 802 us -> 0 us
  Pallas kernels: 0 us -> 251 us
  matrix products: 62.4 us -> 0 us
  starting transfers between devices: 40.5 us -> 0 us
  other arithmetic: 40.3 us -> 0.84 us
  local copies, waits for them, and re-layouts: 45.1 us -> 17.5 us
  between operations: 19.7 us -> 0.71 us
  loops' own time: 15.1 us -> 0 us
    psum x2 -> x0, waiting for transfers between devices: 656 us -> none  [the longest x1 555 us: shards(): summed = lax.psum((grad_w_in, grad_w_out), 'seq')]
    pallas_call x0 -> x3, Pallas kernels: none -> 251 us  [the longest x1 143 us: gradients(): pl.pallas_call(gradient_kernel, out_shape=(jax.ShapeDtypeStruct((T, HALF)...]
    ppermute x16 -> x0, waiting for transfers between devices: 97.4 us -> none  [passed_along(): return lax.ppermute(block, axis, route)]
    dot_general x17 -> x0, matrix products: 59.7 us -> none  [the longest x2 12.5 us: back_some(): jnp.einsum('ihe,jhe->hij', grad_rows, value_rows, preferred_element_type=...]
    ppermute x16 -> x0, starting transfers between devices: 40 us -> none  [passed_along(): return lax.ppermute(block, axis, route)]
    all_gather x2 -> x0, waiting for transfers between devices: 26.2 us -> none  [the longest x1 26.1 us: shards(): lax.all_gather(tokens, 'col', axis=1, tiled=True)]
    reduce_scatter x1 -> x0, waiting for transfers between devices: 20.9 us -> none  [shards(): lax.psum_scatter(out_part.astype(jnp.bfloat16), 'col', scatter_dimension=...]
    cond x10 -> x0, local copies, waits for them, and re-layouts: 19.7 us -> none  [the longest x9 17.1 us: shards(): lax.cond(active, back_some, back_skip, (query_part, key_far, value_far, g...]
  transfers between devices with their start and end apart: 21 -> 0, of which waited for: 12 -> 0; matrix products, arithmetic and copies ran while one was open for 9% -> 0% of each run, Pallas kernels for 0% -> 0%
where the time goes in v1:
time: 270 us
  Pallas kernels  251 us (93%)
  local copies, waits for them, and re-layouts  17.5 us (6%)
    pallas_call x1, Pallas kernels, gradients(): pl.pallas_call(gradient_kernel, out_shape=(jax.ShapeDtypeStruct((T, HALF)...  143 us
    pallas_call x1, Pallas kernels, project(): pl.pallas_call(project_kernel, out_shape=(jax.ShapeDtypeStruct((R, D), BF...  84.7 us
    pallas_call x1, Pallas kernels, attention(): pl.pallas_call(attention_kernel, out_shape=(jax.ShapeDtypeStruct((2, R, H...  23.7 us
    reshape x2, local copies, waits for them, and re-layouts, shards(): gwi = gw[:, :D].reshape(2, D, 4, E).transpose(1, 2, 0, 3)  6.38 us

profile of v1, /device:TPU:1, one launch (start us, length us, event | category | flops | bytes accessed | tf_op | source)
XLA Modules:
  0.0 269.9 jit_solution(18408998297852507089)
XLA Ops:
  0.6 0.0 copy-start
  0.7 0.8 pad_dynamic-slice_fusion
  1.5 0.0 copy-start.3
  1.5 0.1 slice.9
  1.6 0.2 convert_reduce_fusion
  1.8 0.6 and_select_fusion.lo_ref
  2.4 1.6 dynamic-slice_bitcast_fusion.wo_ref
  4.0 0.0 copy-done
  4.0 1.1 constant_dynamic-slice_fusion
  5.0 1.3 copy.18
  6.4 1.0 copy.16.w_ref
  7.4 0.0 copy-done.3
  7.4 84.7 %gather_project.1 = (bf16[2048,512]{1,0:T(8,128)(2,1)}, f32[2048,128]{1,0:T(8,128)}, bf16[2048,128]{1,0:T(8,128)(2,1)}, bf16[2048,128]{1,0:T(8,128)(2,1)}, bf16[...) custom-call(bf16[1024,256]{1,0:T(8,128)(2,1)} %tok_ref.3, bf16[1024,256]{1,0:T(8,128)(2,1)} %cot_ref.3, ...), custom_call_target="tpu_custom_call" | custom-call | flops 1073741824 | bytes 16777216 | tf_op jit(solution)/shard_map/gather_project/pallas_call | solution.py:164
  92.1 23.7 %attention.1 = (bf16[2,2048,256]{2,1,0:T(8,128)(2,1)}, bf16[2048,128]{1,0:T(8,128)(2,1)}, f32[2048,128]{1,0:T(8,128)}, f32[2048,128]{1,0:T(8,128)}, f32[2048,256]{1,0:T(8,128)}, /*index=5*/bf16[2,2048,256]{2,1,0:T(8,128)(2,1)}) custom-call(s32[4]{0:T(128)} %and_select_fusion.lo_ref, bf16[2048,128]{1,0:T(8,128)(2,1)} %get-tuple-element.22.q_ref, ...), custom_call_target="tpu_custom_call" | custom-call | flops 15032385536 | bytes 16777216 | tf_op jit(solution)/shard_map/attention/pallas_call | solution.py:290
  115.8 142.5 %gradients.1 = (bf16[1024,256]{1,0:T(8,128)(2,1)}, bf16[1024,256]{1,0:T(8,128)(2,1)}, f32[2,640,512]{2,1,0:T(8,128)}) custom-call(bf16[1024,256]{1,0:T(8,128)(2,1)} %tok_ref.3, bf16[1024,256]{1,0:T(8,128)(2,1)} %cot_ref.3, bf16[512,512]{1,0:T(8,128)(2,1)} %copy.16.w_ref, bf16[2048,512]{1,0:T(8,128)(2,1)} %get-tuple-element.19.nb_ref, ...), custom_call_target="tpu_custom_call" | custom-call | flops 3758096384 | bytes 16777216 | tf_op jit(solution)/shard_map/gradients/pallas_call | solution.py:496
  258.3 1.9 slice.11
  260.2 1.8 slice.10
  261.9 1.8 reshape.23
  263.7 0.0 copy-start.2
  263.7 0.0 copy-start.1
  263.7 4.6 %copy.20 = f32[2,512,4,128]{3,0,2,1:T(2,128)} copy(f32[2,512,4,128]{3,2,1,0:T(4,128)} %reshape.23) | data formatting | bytes 4194304 | tf_op jit(solution)/shard_map/reshape | solution.py:558
  268.3 0.0 copy-done.2
  268.3 0.8 copy.23
  269.1 0.0 copy-done.1
  269.1 0.8 copy.24
Async XLA Ops:
  0.6 3.3 %copy-start = (bf16[512,4,2,128]{3,2,1,0:T(2,128)(2,1)S(1)}, bf16[512,4,2,128]{3,2,1,0:T(2,128)(2,1)}, u32[]{:S(2)}) copy-start(bf16[512,4,2,128]{3,2,1,0:T(2,128)(2,1)} %param.7) | copy-start | bytes 3145732
  1.5 5.9 %copy-start.3 = (s32[6144]{0:T(1024)}, s32[6144]{0:T(1024)S(1)}, u32[]{:S(2)}) copy-start(s32[6144]{0:T(1024)S(1)} %pad_dynamic-slice_fusion) | copy-start | bytes 73732
  263.7 4.6 %copy-start.2 = (bf16[1024,256]{1,0:T(8,128)(2,1)S(1)}, bf16[1024,256]{1,0:T(8,128)(2,1)}, u32[]{:S(2)}) copy-start(bf16[1024,256]{1,0:T(8,128)(2,1)} %get-tuple-element.38) | copy-start | bytes 1572868
  263.7 5.4 %copy-start.1 = (bf16[1024,256]{1,0:T(8,128)(2,1)S(1)}, bf16[1024,256]{1,0:T(8,128)(2,1)}, u32[]{:S(2)}) copy-start(bf16[1024,256]{1,0:T(8,128)(2,1)} %get-tuple-element.39) | copy-start | bytes 1572868

commit v2 on v1

v2 whole, which is shorter than its diff:
```python
import functools
import math

import jax
import jax.numpy as jnp
from jax import lax
from jax.experimental import pallas as pl
from jax.experimental.pallas import tpu as pltpu
from jax.sharding import PartitionSpec as P

MESH = pl.DeviceIdType.MESH
F32 = jnp.float32
BF16 = jnp.bfloat16

T = 1024
R = 2 * T
D = 512
E = 128
HALF = D // 2
CH = 256
NCH = T // CH
TQ = 512
TK = 512
WIN = 3 * R
EPS = 1e-5
FLOOR = 1.0
SCALE = E**-0.5
OUT_OF_MASK = -32.0
SLOTS = R // CH
AROUND = (0, 1, 2, 4, 6)
CHIPS = 32
VMEM_LIMIT = 56 * 1024 * 1024

NT = (((1,), (1,)), ((), ()))
TN = (((0,), (0,)), ((), ()))


def dot(a, b, dims=(((1,), (0,)), ((), ()))):
    return lax.dot_general(a, b, dims, preferred_element_type=F32)


def guarded(on, act):
    if on is None:
        act()
    else:
        pl.when(on)(act)


class Copy:
    def __init__(self, src, dst, sems, at, device, on=None, arrives=None):
        self.on, self.arrives = on, arrives
        self.copy = pltpu.make_async_remote_copy(
            src_ref=src,
            dst_ref=dst,
            send_sem=sems[0].at[at],
            recv_sem=sems[1].at[at],
            device_id=device,
            device_id_type=MESH,
        )

    def start(self):
        guarded(self.on, self.copy.start)
        return self

    def wait_recv(self):
        guarded(self.arrives, self.copy.wait_recv)

    def wait_send(self):
        guarded(self.on, self.copy.wait_send)


def rows_at(start, size):
    return pl.ds(pl.multiple_of(start, size), size)


class Place:
    def __init__(self):
        s, c = lax.axis_index("seq"), lax.axis_index("col")
        self.s, self.c = s, c
        self.core = lax.rem(s, 2)
        self.chip = lax.div(s, 2)
        self.y = lax.rem(self.chip, 4)
        self.z = lax.rem(lax.div(s, 8), 4)
        self.xl = lax.div(s, 32)
        self.other = (s + 1 - 2 * self.core, c)
        aside = s + 32 - 64 * self.xl
        same = self.xl == 0
        self.xplus = (aside, jnp.where(same, c, 1 - c))
        self.xminus = (aside, jnp.where(same, 1 - c, c))
        self.xpeer = (aside, c)

    def at_chip(self, chip):
        return (2 * lax.rem(chip + 2 * CHIPS, CHIPS) + self.core, self.c)

    def in_ring(self, step):
        return self.chip - self.y + lax.rem(self.y + 4 + step, 4)


def greet(senders, count):
    barrier = pltpu.get_barrier_semaphore()
    for device in senders:
        pl.semaphore_signal(barrier, inc=1, device_id=device, device_id_type=MESH)
    pl.semaphore_wait(barrier, count)


class Across:
    def __init__(self, me, src, via, dst, sems, at, turn):
        first = me.xplus if turn % 2 == 0 else me.xminus
        self.leg = Copy(src, via, sems, at + (0,), first)
        self.next = Copy(via, dst(first[1]), sems, at + (1,), first)

    def start(self):
        self.leg.start()
        return self

    def hand_on(self):
        self.leg.wait_recv()
        self.next.start()

    def wait_recv(self):
        self.next.wait_recv()

    def wait_send(self):
        self.leg.wait_send()
        self.next.wait_send()


def project_kernel(
    tok_ref, cot_ref, w_ref,
    wh_ref, nb_ref, rs_ref, q_ref, up_ref, kv_ref, cg_ref,
    xg, xvia, yvia, wf, xss, xrs, oss, ors, kss, krs,
):
    me = Place()
    c, core, chip = me.c, me.core, me.chip
    ahead = me.at_chip(chip + 1)
    round_to = me.at_chip(me.in_ring(-1))
    source = me.in_ring(1)
    handed_to = me.at_chip(source + 2)
    two_back = lax.rem(chip + CHIPS - 2, CHIPS)
    two_y = lax.rem(two_back, 4)
    hander = me.at_chip(two_back - two_y + lax.rem(two_y + 3, 4))
    greet(
        [me.other, me.xplus, me.xminus, me.at_chip(chip - 1), me.at_chip(source), hander],
        6,
    )

    base = core * T
    obase = (1 - core) * T

    bufs = (xg, cg_ref)
    srcs = (tok_ref, cot_ref)
    x_copies, o_copies, f_copies = {}, {}, {}
    for kind in (0, 1):
        for i in range(NCH):
            rr = rows_at(base + i * CH, CH)
            x_copies[kind, i] = Across(
                me, srcs[kind].at[pl.ds(i * CH, CH)], xvia.at[kind, i],
                lambda col, kind=kind, rr=rr: bufs[kind].at[1 - col, rr],
                (xss, xrs), (kind, i), i,
            )
            o_copies[kind, i] = Copy(
                srcs[kind].at[pl.ds(i * CH, CH)], bufs[kind].at[c, rr], (oss, ors), (kind, 0, i), me.other
            )
            where = bufs[kind].at[1 - c, rr]
            f_copies[kind, i] = Copy(where, where, (oss, ors), (kind, 1, i), me.other)

    for i in range(NCH):
        x_copies[0, i].start()
        o_copies[0, i].start()
    for i in range(NCH):
        xg[c, rows_at(base + i * CH, CH)] = tok_ref[pl.ds(i * CH, CH)]
        cg_ref[c, rows_at(base + i * CH, CH)] = cot_ref[pl.ds(i * CH, CH)]

    wf[...] = w_ref[...].astype(F32)
    for place, part in enumerate((0, 2, 1, 3)):
        lanes = slice(place * E, (place + 1) * E)
        first = wf[pl.ds(2 * part, D, stride=8), :]
        second = wf[pl.ds(2 * part + 1, D, stride=8), :]
        wh_ref[:, lanes] = jnp.where(core == 0, first, second).astype(BF16)

    near, hop, direct, chained = {}, {}, {}, {}
    for slot in range(SLOTS):
        rr = rows_at((base if slot < NCH else obase) + slot % NCH * CH, CH)
        mine = kv_ref.at[2, rr]
        near[slot] = Copy(
            mine, kv_ref.at[1, rr], (kss, krs), (0, slot), ahead, chip < CHIPS - 1, chip > 0
        )
        if slot in AROUND:
            hop[slot] = Copy(
                mine, yvia.at[slot], (kss, krs), (1, slot), round_to,
                chip < CHIPS - 2, source < CHIPS - 2,
            )
            direct[slot] = Copy(
                yvia.at[slot], kv_ref.at[0, rr], (kss, krs), (2, slot), handed_to,
                source < CHIPS - 2, chip > 1,
            )
        else:
            chained[slot] = Copy(
                kv_ref.at[1, rr], kv_ref.at[0, rr], (kss, krs), (2, slot), ahead,
                (chip > 0) & (chip < CHIPS - 1), chip > 1,
            )

    def compute(slot):
        rr = rows_at((base if slot < NCH else obase) + slot % NCH * CH, CH)
        x0 = xg[0, rr].astype(F32)
        x1 = xg[1, rr].astype(F32)
        mean = (jnp.sum(x0, -1, keepdims=True) + jnp.sum(x1, -1, keepdims=True)) * (1.0 / D)
        x0 = x0 - mean
        x1 = x1 - mean
        var = (
            jnp.sum(x0 * x0, -1, keepdims=True) + jnp.sum(x1 * x1, -1, keepdims=True)
        ) * (1.0 / D)
        inv = lax.rsqrt(var + EPS)
        n0 = (x0 * inv).astype(BF16)
        n1 = (x1 * inv).astype(BF16)
        nb_ref[rr, :HALF] = n0
        nb_ref[rr, HALF:] = n1
        rs_ref[rr] = jnp.broadcast_to(inv, (CH, E))
        half = 0.5 * (dot(n0, wh_ref[:HALF]) + dot(n1, wh_ref[HALF:]))
        proj = (half + half * jnp.tanh(half)).astype(BF16)
        up_ref[rr] = proj[:, :E]
        q_ref[rr] = proj[:, E : 2 * E]
        kv_ref[2, rr] = proj[:, 2 * E :]
        near[slot].start()
        if slot in AROUND:
            hop[slot].start()

    def hand_on(slot):
        if slot in AROUND:
            hop[slot].wait_recv()
            direct[slot].start()
        else:
            near[slot].wait_recv()
            chained[slot].start()

    x_copies[0, 0].hand_on()
    for i in range(NCH):
        if i < NCH - 1:
            x_copies[0, i + 1].hand_on()
        x_copies[0, i].wait_recv()
        f_copies[0, i].start()
        compute(i)
        o_copies[0, i].wait_recv()
        f_copies[0, i].wait_recv()
        compute(NCH + i)
        if i == 1:
            for j in range(NCH):
                x_copies[1, j].start()
                o_copies[1, j].start()
        if i:
            hand_on(i - 1)
            hand_on(NCH + i - 1)
    for i in range(NCH):
        x_copies[1, i].hand_on()
    hand_on(NCH - 1)
    hand_on(SLOTS - 1)
    for i in range(NCH):
        x_copies[1, i].wait_recv()
        f_copies[1, i].start()
    for i in range(NCH):
        o_copies[1, i].wait_recv()
        f_copies[1, i].wait_recv()
    for slot in range(SLOTS):
        if slot in AROUND:
            near[slot].wait_recv()
            direct[slot].wait_recv()
        else:
            chained[slot].wait_recv()
    for copies in (x_copies, o_copies, f_copies, near, hop, direct, chained):
        for copy in copies.values():
            copy.wait_send()


def project(tokens, cotangent, w):
    vm = pl.BlockSpec(memory_space=pltpu.VMEM)
    dma = pltpu.SemaphoreType.DMA
    return pl.pallas_call(
        project_kernel,
        out_shape=(
            jax.ShapeDtypeStruct((D, 4 * E), BF16),
            jax.ShapeDtypeStruct((R, D), BF16),
            jax.ShapeDtypeStruct((R, E), F32),
            jax.ShapeDtypeStruct((R, E), BF16),
            jax.ShapeDtypeStruct((R, E), BF16),
            jax.ShapeDtypeStruct((3, R, 2 * E), BF16),
            jax.ShapeDtypeStruct((2, R, HALF), BF16),
        ),
        in_specs=[vm] * 3,
        out_specs=(vm,) * 7,
        scratch_shapes=[
            pltpu.VMEM((2, R, HALF), BF16),
            pltpu.VMEM((2, NCH, CH, HALF), BF16),
            pltpu.VMEM((SLOTS, CH, 2 * E), BF16),
            pltpu.VMEM((8 * D, E), F32),
            dma((2, NCH, 2)),
            dma((2, NCH, 2)),
            dma((2, 2, NCH)),
            dma((2, 2, NCH)),
            dma((3, SLOTS)),
            dma((3, SLOTS)),
        ],
        compiler_params=pltpu.CompilerParams(
            collective_id=0, has_side_effects=True, vmem_limit_bytes=VMEM_LIMIT
        ),
        cost_estimate=pl.CostEstimate(
            flops=2 * R * D * D, bytes_accessed=16 << 20, transcendentals=R * D
        ),
        name="gather_project",
    )(tokens, cotangent, w)


def attention_kernel(
    q_ref, kv_ref, up_ref, cg_ref, wo_all, all_ids,
    op_ref, gated_ref, dup_ref, dq_ref, dkv_ref, dfar_ref,
    id_ref, idc, acc,
):
    s = lax.axis_index("seq")
    chip = lax.div(s, 2)
    wo_ref = wo_all.at[lax.rem(s, 2)]
    windows = []
    for b in range(3):
        source = chip - 2 + b
        ids = all_ids[rows_at(jnp.maximum(source, 0) * (R // E), R // E), :]
        ids = jnp.where(source >= 0, ids, -1)
        windows.append(ids)
        for j in range(R // E):
            at = b * R + j * E
            row = ids[j : j + 1, :]
            id_ref[0:1, at : at + E] = row
            idc[at : at + E, :] = jnp.broadcast_to(row, (E, E)).T

    @pl.loop(0, WIN // TK)
    def _(j):
        acc[rows_at(j * TK, TK), :] = jnp.zeros((TK, 2 * E), F32)

    def spread(column, width):
        return jnp.concatenate([column] * (width // E), axis=1)

    first = 2 * R // TK

    @pl.loop(0, R // TQ)
    def _(t):
        rr = rows_at(t * TQ, TQ)
        q = q_ref[rr, :]
        wr = rows_at(2 * R + t * TQ, TQ)
        idq_col = idc[wr, :]
        idq_row = id_ref[0:1, wr]
        start = idq_row[0, 0]
        low = sum(jnp.sum((ids < start).astype(jnp.int32)) for ids in windows) // TK
        last = first + t * TQ // TK

        def forward(kt, total, causal):
            kr = rows_at(kt * TK, TK)
            half = dot(q, kv_ref[kr, E:], NT) * (0.5 * SCALE)
            ok = spread(idq_col, TK) == id_ref[0:1, kr]
            if causal:
                ri = lax.broadcasted_iota(jnp.int32, (TQ, TK), 0)
                ci = lax.broadcasted_iota(jnp.int32, (TQ, TK), 1)
                ok = ok & (ci <= ri)
            half = jnp.where(ok, half, OUT_OF_MASK)
            weights = (half + half * jnp.tanh(half)).astype(BF16)
            return total + dot(weights, kv_ref[kr, :E])

        att = lax.fori_loop(
            low, last, functools.partial(forward, causal=False), jnp.zeros((TQ, E), F32)
        )
        att = forward(last, att, True)

        center = att - jnp.mean(att, -1, keepdims=True)
        scale = lax.rsqrt(jnp.mean(center * center, -1, keepdims=True) + FLOOR)
        hn = center * scale
        up = up_ref[rr, :].astype(F32)
        gated = (hn * up).astype(BF16)
        gated_ref[rr, :] = gated
        op_ref[0, rr, :] = dot(gated, wo_ref[:, :HALF]).astype(BF16)
        op_ref[1, rr, :] = dot(gated, wo_ref[:, HALF:]).astype(BF16)
        gg = dot(cg_ref[0, rr, :], wo_ref[:, :HALF], NT) + dot(cg_ref[1, rr, :], wo_ref[:, HALF:], NT)
        dup_ref[rr, :] = gg * hn
        b = gg * up
        grad = (
            scale
            * (b - jnp.mean(b, -1, keepdims=True) - hn * jnp.mean(b * hn, -1, keepdims=True))
        ).astype(BF16)

        def backward(kt, total, causal):
            kr = rows_at(kt * TK, TK)
            k = kv_ref[kr, E:]
            half = dot(k, q, NT) * (0.5 * SCALE)
            ok = spread(idc[kr, :], TQ) == idq_row
            if causal:
                ri = lax.broadcasted_iota(jnp.int32, (TK, TQ), 0)
                ci = lax.broadcasted_iota(jnp.int32, (TK, TQ), 1)
                ok = ok & (ri <= ci)
            half = jnp.where(ok, half, OUT_OF_MASK)
            tan = jnp.tanh(half)
            weights = half + half * tan
            tan = 0.5 * tan
            slope = (0.5 + tan) + weights * (0.5 - tan)
            ds = (slope * dot(kv_ref[kr, :E], grad, NT)).astype(BF16)
            acc[kr, E:] += dot(ds, q)
            acc[kr, :E] += dot(weights.astype(BF16), grad)
            return total + dot(ds, k, TN)

        dq = lax.fori_loop(
            low, last, functools.partial(backward, causal=False), jnp.zeros((TQ, E), F32)
        )
        dq_ref[rr, :] = backward(last, dq, True) * SCALE

    @pl.loop(0, R // TK)
    def _(j):
        rr = rows_at(j * TK, TK)
        own = rows_at(2 * R + j * TK, TK)
        dkv_ref[rr, :E] = acc[own, :E]
        dkv_ref[rr, E:] = acc[own, E:] * SCALE
        for k in range(2):
            src = rows_at(k * R + j * TK, TK)
            dfar_ref[k, rr, :E] = acc[src, :E].astype(BF16)
            dfar_ref[k, rr, E:] = (acc[src, E:] * SCALE).astype(BF16)


def attention(q, kv, up, cg, wo, ids):
    vm = pl.BlockSpec(memory_space=pltpu.VMEM)
    return pl.pallas_call(
        attention_kernel,
        out_shape=(
            jax.ShapeDtypeStruct((2, R, HALF), BF16),
            jax.ShapeDtypeStruct((R, E), BF16),
            jax.ShapeDtypeStruct((R, E), F32),
            jax.ShapeDtypeStruct((R, E), F32),
            jax.ShapeDtypeStruct((R, 2 * E), F32),
            jax.ShapeDtypeStruct((2, R, 2 * E), BF16),
        ),
        in_specs=[vm] * 6,
        out_specs=(vm,) * 6,
        scratch_shapes=[
            pltpu.VMEM((1, WIN), jnp.int32),
            pltpu.VMEM((WIN, E), jnp.int32),
            pltpu.VMEM((WIN, 2 * E), F32),
        ],
        compiler_params=pltpu.CompilerParams(vmem_limit_bytes=VMEM_LIMIT),
        cost_estimate=pl.CostEstimate(
            flops=7 * 2 * R * R * 2 * E, bytes_accessed=16 << 20, transcendentals=4 * R * R
        ),
        name="attention",
    )(q, kv, up, cg, wo, ids)


class Summed:
    def __init__(self, me, rows, grads, bufs, sems, at):
        self.me, self.rows, self.grads, self.bufs = me, rows, grads, bufs
        self.sems, self.at = sems, at
        self.done = []

    def copy(self, src, dst, stage, k, device):
        copy = Copy(src, dst, self.sems, (self.at, stage, k), device).start()
        self.done.append(copy)
        return copy

    def peers(self, here, step):
        s, c = self.me.s, self.me.c
        there = [lax.rem(here + k, 4) for k in (1, 2, 3)]
        return [(v, (s + step * (v - here), c)) for v in there]

    def start(self):
        zbuf, zrecv = self.bufs[0:2]
        n = self.rows // 4
        zbuf[...] = self.grads[...].astype(BF16)
        self.zc = [
            self.copy(zbuf.at[rows_at(v * n, n)], zrecv.at[k], 0, k, device)
            for k, (v, device) in enumerate(self.peers(self.me.z, 8))
        ]

    def over_y(self):
        zrecv, yacc, ybuf, yrecv = self.bufs[1:5]
        n, m = self.rows // 4, self.rows // 16
        for copy in self.zc:
            copy.wait_recv()
        total = self.grads[rows_at(self.me.z * n, n), :]
        for k in range(3):
            total = total + zrecv[k].astype(F32)
        yacc[...] = total
        ybuf[...] = total.astype(BF16)
        self.yc = [
            self.copy(ybuf.at[rows_at(v * m, m)], yrecv.at[k], 1, k, device)
            for k, (v, device) in enumerate(self.peers(self.me.y, 2))
        ]

    def over_x(self):
        yacc, _, yrecv, xacc, xbuf, xrecv = self.bufs[2:8]
        m = self.rows // 16
        for copy in self.yc:
            copy.wait_recv()
        total = yacc[rows_at(self.me.y * m, m), :]
        for k in range(3):
            total = total + yrecv[k].astype(F32)
        for j in range(2):
            xacc[j] = total[:, j * E : (j + 1) * E]
            xbuf[j] = total[:, j * E : (j + 1) * E].astype(BF16)
        self.xc = self.copy(xbuf.at[1 - self.me.xl], xrecv, 2, 0, self.me.xpeer)

    def back_x(self):
        xacc, _, xrecv, whole = self.bufs[5:9]
        me = self.me
        self.xc.wait_recv()
        spot = whole.at[me.core, me.z, me.y, me.xl]
        spot[...] = (xacc[me.xl] + xrecv[...].astype(F32)).astype(BF16)
        self.gx = self.copy(spot, spot, 3, 0, me.xpeer)

    def back_y(self):
        me = self.me
        self.gx.wait_recv()
        spot = self.bufs[8].at[me.core, me.z, me.y]
        self.gy = [
            self.copy(spot, spot, 4, k, device) for k, (_, device) in enumerate(self.peers(me.y, 2))
        ]

    def back_z(self):
        me = self.me
        for copy in self.gy:
            copy.wait_recv()
        spot = self.bufs[8].at[me.core, me.z]
        self.gz = [
            self.copy(spot, spot, 5, k, device) for k, (_, device) in enumerate(self.peers(me.z, 8))
        ]
        self.gc = [self.copy(spot, spot, 6, 0, me.other)]

    def back_core(self):
        me = self.me
        for k in range(3):
            self.gz[k].wait_recv()
            spot = self.bufs[8].at[me.core, lax.rem(me.z + 3 - k, 4)]
            self.gc.append(self.copy(spot, spot, 6, k + 1, me.other))

    def finish(self):
        for copy in self.gc:
            copy.wait_recv()

    def wait_send(self):
        for copy in self.done:
            copy.wait_send()

    @staticmethod
    def scratch(rows):
        n, m = rows // 4, rows // 16
        return [
            pltpu.VMEM((rows, 2 * E), BF16),
            pltpu.VMEM((3, n, 2 * E), BF16),
            pltpu.VMEM((n, 2 * E), F32),
            pltpu.VMEM((n, 2 * E), BF16),
            pltpu.VMEM((3, m, 2 * E), BF16),
            pltpu.VMEM((2, m, E), F32),
            pltpu.VMEM((2, m, E), BF16),
            pltpu.VMEM((m, E), BF16),
            pltpu.VMEM((2, 4, 4, 2, m, E), BF16),
        ]


EARLY = D + 2 * E
INV_ROOT = 1.0 / 256.0


def gradient_kernel(
    tok_ref, cot_ref, w_ref, nb_ref, rs_ref, cg_ref, gated_ref, op_ref, dup_ref, dq_ref, dkv_ref, dfar_ref,
    out_ref, gt_ref, gwi_ref, gwo_ref,
    hopped, back, yvia, slope, gp, part, chip_sum, to_col, xvia, from_col, early_g, late_g, *rest,
):
    early_bufs, late_bufs = rest[:9], rest[9:18]
    bss, brs, sss, srs, xss, xrs, ass, ars = rest[18:]
    me = Place()
    c, core, chip = me.c, me.core, me.chip
    behind = me.at_chip(chip - 1)
    round_to = me.at_chip(me.in_ring(1))
    source = me.in_ring(-1)
    handed_to = me.at_chip(source - 2)
    two_on = lax.rem(chip + 2, CHIPS)
    two_y = lax.rem(two_on, 4)
    hander = me.at_chip(two_on - two_y + lax.rem(two_y + 1, 4))
    early = Summed(me, EARLY, early_g, early_bufs, (ass, ars), 0)
    late = Summed(me, D, late_g, late_bufs, (ass, ars), 1)
    greet(
        [me.other, me.xplus, me.xminus, me.at_chip(chip + 1), me.at_chip(source), hander, me.xpeer]
        + [device for _, device in early.peers(me.y, 2) + early.peers(me.z, 8)],
        13,
    )

    base = core * T
    obase = (1 - core) * T

    def to_core(kind, i):
        src = (op_ref, part)[kind].at[:, rows_at(obase + i * CH, CH)]
        dst = chip_sum.at[kind, :, pl.ds(i * CH, CH)]
        return Copy(src, dst, (sss, srs), (kind, i), me.other).start()

    def across(kind, i, copy):
        copy.wait_recv()
        src = (op_ref, part)[kind]
        here = pl.ds(i * CH, CH)
        mine = src[1 - c, rows_at(base + i * CH, CH)].astype(F32)
        to_col[kind, here] = (mine + chip_sum[kind, 1 - c, here].astype(F32)).astype(BF16)
        return Across(
            me, to_col.at[kind, here], xvia.at[kind, i], lambda col: from_col.at[kind, here],
            (xss, xrs), (kind, i), i,
        ).start()

    def finish(kind, i, copy):
        copy.wait_recv()
        here = pl.ds(i * CH, CH)
        src, own, out = ((op_ref, tok_ref, out_ref), (part, cot_ref, gt_ref))[kind]
        total = src[c, rows_at(base + i * CH, CH)].astype(F32)
        total = total + chip_sum[kind, c, here].astype(F32)
        total = total + from_col[kind, here].astype(F32)
        out[here] = (own[here].astype(F32) + total).astype(BF16)

    near, hop, direct = {}, {}, {}
    for i in range(SLOTS):
        rr = pl.ds(i * CH, CH)
        near[i] = Copy(
            dfar_ref.at[1, rr] if i in AROUND else back.at[2, rr], back.at[1, rr], (bss, brs), (0, i), behind,
            chip > 0, chip < CHIPS - 1,
        )
        if i in AROUND:
            hop[i] = Copy(
                dfar_ref.at[0, rr], yvia.at[i], (bss, brs), (1, i), round_to, chip > 1, source > 1
            )
            direct[i] = Copy(
                yvia.at[i], back.at[0, rr], (bss, brs), (2, i), handed_to, source > 1, chip < CHIPS - 2
            )
        else:
            hop[i] = Copy(
                dfar_ref.at[0, rr], hopped.at[i], (bss, brs), (1, i), behind,
                chip > 1, (chip > 0) & (chip < CHIPS - 1),
            )
        hop[i].start()
        if i in AROUND:
            near[i].start()
    out_core = [to_core(0, i) for i in range(NCH)]

    SR = 512

    @pl.loop(0, R // SR)
    def _(i):
        rr = rows_at(i * SR, SR)
        half = 0.5 * dot(nb_ref[rr, :], w_ref[...])
        tan = jnp.tanh(half)
        silu = half + half * tan
        tan = 0.5 * tan
        sl = (0.5 + tan) + silu * (0.5 - tan)
        gp[rr, :E] = (dup_ref[rr, :] * sl[:, :E]).astype(BF16)
        gp[rr, E : 2 * E] = (dq_ref[rr, :] * sl[:, E : 2 * E]).astype(BF16)
        slope[rr, :] = sl[:, 2 * E :]

    early_g[:D, :] = dot(nb_ref[...], gp[:, : 2 * E], TN)
    for j in range(2):
        early_g[D + j * E : D + (j + 1) * E, :] = dot(gated_ref[...], cg_ref[j], TN)
    early.start()

    out_far = [across(0, i, out_core[i]) for i in range(NCH)]

    for i in range(SLOTS):
        rr = pl.ds(i * CH, CH)
        if i in AROUND:
            hop[i].wait_recv()
            direct[i].start()
        else:
            back[2, rr] = dfar_ref[1, rr]

            @pl.when((chip > 0) & (chip < CHIPS - 1))
            def _():
                hop[i].copy.wait_recv()
                back[2, rr] = (dfar_ref[1, rr].astype(F32) + hopped[i].astype(F32)).astype(BF16)

            near[i].start()
    for copy in out_far:
        copy.hand_on()
    early.over_y()

    for i in range(SLOTS):
        rr = pl.ds(i * CH, CH)
        near[i].wait_recv()

        @pl.when(chip == CHIPS - 1)
        def _():
            back[1, rr] = jnp.zeros((CH, 2 * E), BF16)

        g = dkv_ref[rr, :]
        if i in AROUND:
            direct[i].wait_recv()

            @pl.when(chip >= CHIPS - 2)
            def _():
                back[0, rr] = jnp.zeros((CH, 2 * E), BF16)

            g = g + back[0, rr].astype(F32)
        gp[rr, 2 * E :] = ((g + back[1, rr].astype(F32)) * slope[rr, :]).astype(BF16)

    late_g[...] = dot(nb_ref[...], gp[:, 2 * E :], TN)
    late.start()
    early.over_x()

    def tokens_back(start):
        rr = rows_at(start, CH)
        g = dot(gp[rr, :], w_ref[...], NT)
        nb = nb_ref[rr, :].astype(F32)
        inv = rs_ref[rr, 0:1]
        g = inv * (g - jnp.mean(g, -1, keepdims=True) - nb * jnp.mean(g * nb, -1, keepdims=True))
        part[0, rr] = g[:, :HALF].astype(BF16)
        part[1, rr] = g[:, HALF:].astype(BF16)

    gt_core = []
    for i in range(NCH):
        tokens_back(obase + i * CH)
        gt_core.append(to_core(1, i))
    early.back_x()
    gt_far = []
    for i in range(NCH):
        tokens_back(base + i * CH)
        gt_far.append(across(1, i, gt_core[i]))
    late.over_y()
    early.back_y()
    for copy in gt_far[:2]:
        copy.hand_on()
    late.over_x()
    early.back_z()
    for copy in gt_far[2:]:
        copy.hand_on()
    late.back_x()
    late.back_y()
    early.back_core()
    late.back_z()
    for i in range(NCH):
        finish(0, i, out_far[i])
    early.finish()
    for h in range(2):
        for z in range(4):
            for y in range(4):
                for j in range(2):
                    n = EARLY // 16
                    row = (4 * z + y) * n
                    block = early_bufs[8][h, z, y, j].astype(F32) * INV_ROOT
                    at = 0
                    while at < n:
                        d = row + at
                        end = next(b for b in (D, D + E, EARLY) if b > d)
                        size = min(n - at, end - d)
                        piece = block[at : at + size]
                        if d < D:
                            gwi_ref[pl.ds(8 * d + 4 * j + h, size, stride=8), :] = piece
                        else:
                            q, e = divmod(d - D, E)
                            gwo_ref[h, e : e + size, q * HALF + j * E : q * HALF + (j + 1) * E] = piece
                        at += size
    late.back_core()
    for i in range(NCH):
        finish(1, i, gt_far[i])
    late.finish()
    for h in range(2):
        for z in range(4):
            for y in range(4):
                for j in range(2):
                    n = D // 16
                    row = (4 * z + y) * n
                    gwi_ref[pl.ds(8 * row + 4 * j + 2 + h, n, stride=8), :] = (
                        late_bufs[8][h, z, y, j].astype(F32) * INV_ROOT
                    )
    for copies in (near, hop, direct):
        for copy in copies.values():
            copy.wait_send()
    for copy in out_core + out_far + gt_core + gt_far + [early, late]:
        copy.wait_send()


def gradients(*operands):
    vm = pl.BlockSpec(memory_space=pltpu.VMEM)
    dma = pltpu.SemaphoreType.DMA
    return pl.pallas_call(
        gradient_kernel,
        out_shape=(
            jax.ShapeDtypeStruct((T, HALF), BF16),
            jax.ShapeDtypeStruct((T, HALF), BF16),
            jax.ShapeDtypeStruct((8 * D, E), F32),
            jax.ShapeDtypeStruct((2, E, D), F32),
        ),
        in_specs=[vm] * 12,
        out_specs=(vm,) * 4,
        scratch_shapes=[
            pltpu.VMEM((SLOTS, CH, 2 * E), BF16),
            pltpu.VMEM((3, R, 2 * E), BF16),
            pltpu.VMEM((SLOTS, CH, 2 * E), BF16),
            pltpu.VMEM((R, 2 * E), F32),
            pltpu.VMEM((R, 4 * E), BF16),
            pltpu.VMEM((2, R, HALF), BF16),
            pltpu.VMEM((2, 2, T, HALF), BF16),
            pltpu.VMEM((2, T, HALF), BF16),
            pltpu.VMEM((2, NCH, CH, HALF), BF16),
            pltpu.VMEM((2, T, HALF), BF16),
            pltpu.VMEM((EARLY, 2 * E), F32),
            pltpu.VMEM((D, 2 * E), F32),
        ]
        + Summed.scratch(EARLY)
        + Summed.scratch(D)
        + [
            dma((3, SLOTS)),
            dma((3, SLOTS)),
            dma((2, NCH)),
            dma((2, NCH)),
            dma((2, NCH, 2)),
            dma((2, NCH, 2)),
            dma((2, 7, 4)),
            dma((2, 7, 4)),
        ],
        compiler_params=pltpu.CompilerParams(
            collective_id=1, has_side_effects=True, vmem_limit_bytes=VMEM_LIMIT
        ),
        cost_estimate=pl.CostEstimate(
            flops=7 * R * D * D, bytes_accessed=16 << 20, transcendentals=R * D
        ),
        name="gradients",
    )(*operands)


def shards(tokens, cotangent, weight_in, weight_out, history_ids):
    w, nb, inv, q, up, kv, cg = project(tokens, cotangent, weight_in.reshape(8 * D, E))
    op, gated, dup, dq, dkv, dfar = attention(
        q, kv.reshape(WIN, 2 * E), up, cg, weight_out, history_ids.reshape(-1, E)
    )
    out, gt, gwi, gwo = gradients(
        tokens, cotangent, w, nb, inv, cg, gated, op, dup, dq, dkv, dfar
    )
    return out, gt, gwi.reshape(D, 4, 2, E), gwo


def solution(mesh):
    placed = (
        P("seq", "col"),
        P("seq", "col"),
        P(None, None, "col", None),
        P("col", None, None),
        P(),
    )
    return jax.shard_map(
        shards,
        mesh=mesh,
        in_specs=placed,
        out_specs=(
            P("seq", "col"),
            P("seq", "col"),
            P(None, None, "col", None),
            P("col", None, None),
        ),
        check_vma=False,
    )
```

time: 270 us -> 226 us (0.84)
  Pallas kernels: 251 us -> 219 us
  local copies, waits for them, and re-layouts: 17.5 us -> 6.08 us
    pallas_call x1, Pallas kernels: 84.7 us -> 56.5 us  [project(): pl.pallas_call(project_kernel, out_shape=(jax.ShapeDtypeStruct((D, 4 * E)...]
    reshape x3 -> x0, local copies, waits for them, and re-layouts: 7.38 us -> none  [the longest x2 6.38 us: shards(): gwi = gw[:, :D].reshape(2, D, 4, E).transpose(1, 2, 0, 3)]
    pallas_call x1, Pallas kernels: 143 us -> 135 us  [gradients(): pl.pallas_call(gradient_kernel, out_shape=(jax.ShapeDtypeStruct((T, HALF)...]
    pallas_call x1, Pallas kernels: 23.7 us -> 27.8 us  [attention(): pl.pallas_call(attention_kernel, out_shape=(jax.ShapeDtypeStruct((2, R, H...]
    slice x3 -> x0, local copies, waits for them, and re-layouts: 3.72 us -> none  [the longest x1 1.87 us: shards(): return (out, gt, gwi, gw[:, D:])]
    unnamed x11 -> x8, local copies, waits for them, and re-layouts: 2.93 us -> 6.08 us
where the time goes in v2:
time: 226 us
  Pallas kernels  219 us (97%)
  local copies, waits for them, and re-layouts  6.08 us (3%)
    pallas_call x1, Pallas kernels, gradients(): pl.pallas_call(gradient_kernel, out_shape=(jax.ShapeDtypeStruct((T, HALF)...  135 us
    pallas_call x1, Pallas kernels, project(): pl.pallas_call(project_kernel, out_shape=(jax.ShapeDtypeStruct((D, 4 * E)...  56.5 us
    pallas_call x1, Pallas kernels, attention(): pl.pallas_call(attention_kernel, out_shape=(jax.ShapeDtypeStruct((2, R, H...  27.8 us
    unnamed x8, local copies, waits for them, and re-layouts  6.08 us

profile of v2, /device:TPU:1, one launch (start us, length us, event | category | flops | bytes accessed | tf_op | source)
XLA Modules:
  0.0 226.2 jit_solution(977696462656313378)
XLA Ops:
  0.6 56.5 %gather_project.1 = (bf16[512,512]{1,0:T(8,128)(2,1)}, bf16[2048,512]{1,0:T(8,128)(2,1)}, f32[2048,128]{1,0:T(8,128)}, bf16[2048,128]{1,0:T(8,128)(2,1)}, bf16[2...) custom-call(bf16[1024,256]{1,0:T(8,128)(2,1)} %tok_ref.3, ...), custom_call_target="tpu_custom_call" | custom-call | flops 1073741824 | bytes 16777216 | tf_op jit(solution)/shard_map/gather_project/pallas_call | solution.py:277
  57.1 27.8 %attention.1 = (bf16[2,2048,256]{2,1,0:T(8,128)(2,1)}, bf16[2048,128]{1,0:T(8,128)(2,1)}, f32[2048,128]{1,0:T(8,128)}, f32[2048,128]{1,0:T(8,128)}, f32[2048,256]{1,0:T(8,128)}, /*index=5*/bf16[2,2048,256]{2,1,0:T(8,128)(2,1)}) custom-call(bf16[2048,128]{1,0:T(8,128)(2,1)} %get-tuple-element.25.q_ref, bf16[6144,256]{1,0:T(8,128)(2,1)} %bitcast.7, ...), custom_call_target="tpu_custom_call" | custom-call | flops 15032385536 | bytes 16777216 | tf_op jit(solution)/shard_map/attention/pallas_call | solution.py:423
  84.9 135.2 %gradients.1 = (bf16[1024,256]{1,0:T(8,128)(2,1)}, bf16[1024,256]{1,0:T(8,128)(2,1)}, f32[4096,128]{1,0:T(8,128)}, f32[2,128,512]{2,1,0:T(8,128)}) custom-call(bf16[1024,256]{1,0:T(8,128)(2,1)} %tok_ref.3, bf16[1024,256]{1,0:T(8,128)(2,1)} %cot_ref.3, bf16[512,512]{1,0:T(8,128)(2,1)} %get-tuple-element.21.w_ref, bf16[2048,512]{1,0:T(8,128)(2,1)} %get-tuple-element.22.nb_ref, ...), custom_call_target="tpu_custom_call" | custom-call | flops 3758096384 | bytes 16777216 | tf_op jit(solution)/shard_map/gradients/pallas_call | solution.py:775
  220.1 0.0 copy-start
  220.1 2.0 copy.13
  222.1 1.9 copy.14
  224.0 0.0 copy-done
  224.0 0.0 copy-start.1
  224.0 1.3 copy.15
  225.3 0.1 copy-done.1
  225.4 0.8 copy.16
Async XLA Ops:
  220.1 3.9 %copy-start = (f32[4096,128]{1,0:T(8,128)S(1)}, f32[4096,128]{1,0:T(8,128)}, u32[]{:S(2)}) copy-start(f32[4096,128]{1,0:T(8,128)} %get-tuple-element.36) | copy-start | bytes 6291460
  224.0 1.4 copy-start.1

commit v3 on v2

v3 whole, which is shorter than its diff:
```python
import functools
import math

import jax
import jax.numpy as jnp
from jax import lax
from jax.experimental import pallas as pl
from jax.experimental.pallas import tpu as pltpu
from jax.sharding import PartitionSpec as P

MESH = pl.DeviceIdType.MESH
F32 = jnp.float32
BF16 = jnp.bfloat16

T = 1024
R = 2 * T
D = 512
E = 128
HALF = D // 2
CH = 256
NCH = T // CH
TQ = 512
TK = 512
WIN = 3 * R
EPS = 1e-5
FLOOR = 1.0
SCALE = E**-0.5
OUT_OF_MASK = -32.0
SLOTS = R // CH
AROUND = (2, 3, 5, 6, 7)
CHIPS = 32
VMEM_LIMIT = 56 * 1024 * 1024

NT = (((1,), (1,)), ((), ()))
TN = (((0,), (0,)), ((), ()))


def dot(a, b, dims=(((1,), (0,)), ((), ()))):
    return lax.dot_general(a, b, dims, preferred_element_type=F32)


def guarded(on, act):
    if on is None:
        act()
    else:
        pl.when(on)(act)


class Copy:
    def __init__(self, src, dst, sems, at, device, on=None, arrives=None):
        self.on, self.arrives = on, arrives
        self.copy = pltpu.make_async_remote_copy(
            src_ref=src,
            dst_ref=dst,
            send_sem=sems[0].at[at],
            recv_sem=sems[1].at[at],
            device_id=device,
            device_id_type=MESH,
        )

    def start(self):
        guarded(self.on, self.copy.start)
        return self

    def wait_recv(self):
        guarded(self.arrives, self.copy.wait_recv)

    def wait_send(self):
        guarded(self.on, self.copy.wait_send)


def rows_at(start, size):
    return pl.ds(pl.multiple_of(start, size), size)


class Place:
    def __init__(self):
        s, c = lax.axis_index("seq"), lax.axis_index("col")
        self.s, self.c = s, c
        self.core = lax.rem(s, 2)
        self.chip = lax.div(s, 2)
        self.y = lax.rem(self.chip, 4)
        self.z = lax.rem(lax.div(s, 8), 4)
        self.xl = lax.div(s, 32)
        self.other = (s + 1 - 2 * self.core, c)
        self.far = (s, 1 - c)
        self.xpeer = (s + 32 - 64 * self.xl, c)

    def at_chip(self, chip):
        return (2 * lax.rem(chip + 2 * CHIPS, CHIPS) + self.core, self.c)

    def in_ring(self, step):
        return self.chip - self.y + lax.rem(self.y + 4 + step, 4)


def greet(senders, count):
    barrier = pltpu.get_barrier_semaphore()
    for device in senders:
        pl.semaphore_signal(barrier, inc=1, device_id=device, device_id_type=MESH)
    pl.semaphore_wait(barrier, count)


class Near:
    def __init__(self, me, step, src, via, dst, sems, at):
        edge = 3 if step > 0 else 0
        first, last = (0, CHIPS - 1) if step > 0 else (CHIPS - 1, 0)
        cross = me.y == edge
        goes = me.chip != last
        self.comes = me.chip != first
        self.straight = Copy(src, dst, sems, (0,) + at, me.at_chip(me.chip + step), goes & ~cross, self.comes)
        beyond = me.chip > 3 if step > 0 else me.chip < CHIPS - 4
        self.aside = Copy(
            src, via, sems, (1,) + at, me.at_chip(me.chip + 4 * step), goes & cross, beyond & cross
        )
        self.onward = Copy(via, dst, sems, (0,) + at, me.at_chip(me.in_ring(step)), beyond & cross)

    def start(self):
        self.straight.start()
        self.aside.start()

    def hand_on(self):
        self.aside.wait_recv()
        self.onward.start()

    def wait_recv(self):
        self.straight.wait_recv()

    def wait_send(self):
        for copy in (self.straight, self.aside, self.onward):
            copy.wait_send()


def project_kernel(
    tok_ref, cot_ref, w_ref,
    wh_ref, nb_ref, rs_ref, q_ref, up_ref, kv_ref, cg_ref,
    xg, yvia, nvia, wv, wf, wh, nb, inv_all, qv, upv, cg, oss, ors, kss, krs, ls, lcg,
):
    me = Place()
    c, core, chip = me.c, me.core, me.chip
    ahead = me.at_chip(chip + 1)
    round_to = me.at_chip(me.in_ring(-1))
    source = me.in_ring(1)
    handed_to = me.at_chip(source + 2)
    two_back = lax.rem(chip + CHIPS - 2, CHIPS)
    two_y = lax.rem(two_back, 4)
    hander = me.at_chip(two_back - two_y + lax.rem(two_y + 3, 4))
    greet(
        [me.other, me.far, me.at_chip(chip - 1), me.at_chip(chip - 4), round_to, me.at_chip(source), hander],
        7,
    )

    base = core * T
    obase = (1 - core) * T

    bufs = (xg, cg)
    srcs = (tok_ref, cot_ref)
    x_copies, o_copies, f_copies = {}, {}, {}
    for kind in (0, 1):
        for i in range(NCH):
            rr = rows_at(base + i * CH, CH)
            x_copies[kind, i] = Copy(
                srcs[kind].at[pl.ds(i * CH, CH)], bufs[kind].at[c, rr], (oss, ors), (kind, 2, i), me.far
            )
            o_copies[kind, i] = Copy(
                srcs[kind].at[pl.ds(i * CH, CH)], bufs[kind].at[c, rr], (oss, ors), (kind, 0, i), me.other
            )
            where = bufs[kind].at[1 - c, rr]
            f_copies[kind, i] = Copy(where, where, (oss, ors), (kind, 1, i), me.other)

    for i in range(NCH):
        x_copies[0, i].start()
        o_copies[0, i].start()
    loads = [
        pltpu.make_async_copy(src, dst, lcg.at[k])
        for k, (src, dst) in enumerate(
            (
                (w_ref, wv),
                (tok_ref, xg.at[c, rows_at(base, T)]),
                (cot_ref, cg.at[c, rows_at(base, T)]),
            )
        )
    ]
    for copy in loads:
        copy.start()
    for copy in loads:
        copy.wait()
    stores = []

    def store(k, slot, src, dst):
        copy = pltpu.make_async_copy(src, dst, ls.at[k, slot])
        copy.start()
        stores.append(copy)

    wf[...] = wv[...].astype(F32)
    for place, part in enumerate((0, 2, 1, 3)):
        lanes = slice(place * E, (place + 1) * E)
        first = wf[pl.ds(2 * part, D, stride=8), :]
        second = wf[pl.ds(2 * part + 1, D, stride=8), :]
        wh[:, lanes] = jnp.where(core == 0, first, second).astype(BF16)
    store(4, 0, wh, wh_ref)

    near, hop, direct, chained = {}, {}, {}, {}
    for slot in range(SLOTS):
        rr = rows_at((base if slot < NCH else obase) + slot % NCH * CH, CH)
        mine = kv_ref.at[2, rr]
        near[slot] = Near(me, 1, mine, nvia.at[slot], kv_ref.at[1, rr], (kss, krs), (slot,))
        if slot in AROUND:
            hop[slot] = Copy(
                mine, yvia.at[slot], (kss, krs), (2, slot), round_to,
                chip < CHIPS - 2, source < CHIPS - 2,
            )
            direct[slot] = Copy(
                yvia.at[slot], kv_ref.at[0, rr], (kss, krs), (3, slot), handed_to,
                source < CHIPS - 2, chip > 1,
            )
        else:
            chained[slot] = Copy(
                kv_ref.at[1, rr], kv_ref.at[0, rr], (kss, krs), (3, slot), ahead,
                (chip > 0) & (chip < CHIPS - 1), chip > 1,
            )

    def compute(slot):
        rr = rows_at((base if slot < NCH else obase) + slot % NCH * CH, CH)
        x0 = xg[0, rr].astype(F32)
        x1 = xg[1, rr].astype(F32)
        mean = (jnp.sum(x0, -1, keepdims=True) + jnp.sum(x1, -1, keepdims=True)) * (1.0 / D)
        x0 = x0 - mean
        x1 = x1 - mean
        var = (
            jnp.sum(x0 * x0, -1, keepdims=True) + jnp.sum(x1 * x1, -1, keepdims=True)
        ) * (1.0 / D)
        inv = lax.rsqrt(var + EPS)
        n0 = (x0 * inv).astype(BF16)
        n1 = (x1 * inv).astype(BF16)
        half = 0.5 * (dot(n0, wh[:HALF]) + dot(n1, wh[HALF:]))
        proj = (half + half * jnp.tanh(half)).astype(BF16)
        kv_ref[2, rr] = proj[:, 2 * E :]
        near[slot].start()
        if slot in AROUND:
            hop[slot].start()
        nb[rr, :HALF] = n0
        nb[rr, HALF:] = n1
        inv_all[rr] = jnp.broadcast_to(inv, (CH, E))
        upv[rr] = proj[:, :E]
        qv[rr] = proj[:, E : 2 * E]
        for k, (src, dst) in enumerate(((nb, nb_ref), (inv_all, rs_ref), (upv, up_ref), (qv, q_ref))):
            store(k, slot, src.at[rr], dst.at[rr])

    def hand_on(slot):
        if slot in AROUND:
            hop[slot].wait_recv()
            direct[slot].start()
        else:
            near[slot].wait_recv()
            chained[slot].start()

    for i in range(NCH):
        x_copies[0, i].wait_recv()
        f_copies[0, i].start()
        compute(i)
        o_copies[0, i].wait_recv()
        f_copies[0, i].wait_recv()
        compute(NCH + i)
        if i:
            for slot in (i - 1, NCH + i - 1):
                near[slot].hand_on()
                if slot in AROUND:
                    hand_on(slot)
    for i in range(NCH):
        x_copies[1, i].start()
        o_copies[1, i].start()
    for slot in (NCH - 1, SLOTS - 1):
        near[slot].hand_on()
        if slot in AROUND:
            hand_on(slot)
    for slot in (0, NCH, 1):
        hand_on(slot)
    for i in range(NCH):
        x_copies[1, i].wait_recv()
        f_copies[1, i].start()
    for i in range(NCH):
        o_copies[1, i].wait_recv()
        f_copies[1, i].wait_recv()
    copy = pltpu.make_async_copy(cg, cg_ref, lcg.at[3])
    copy.start()
    stores.append(copy)
    for slot in range(SLOTS):
        if slot in AROUND:
            near[slot].wait_recv()
            direct[slot].wait_recv()
        else:
            chained[slot].wait_recv()
    for copies in (x_copies, o_copies, f_copies, near, hop, direct, chained):
        for copy in copies.values():
            copy.wait_send()
    for copy in stores:
        copy.wait()


def project(tokens, cotangent, w):
    vm = pl.BlockSpec(memory_space=pltpu.VMEM)
    hbm = pl.BlockSpec(memory_space=pl.ANY)
    dma = pltpu.SemaphoreType.DMA
    return pl.pallas_call(
        project_kernel,
        out_shape=(
            jax.ShapeDtypeStruct((D, 4 * E), BF16),
            jax.ShapeDtypeStruct((R, D), BF16),
            jax.ShapeDtypeStruct((R, E), F32),
            jax.ShapeDtypeStruct((R, E), BF16),
            jax.ShapeDtypeStruct((R, E), BF16),
            jax.ShapeDtypeStruct((3, R, 2 * E), BF16),
            jax.ShapeDtypeStruct((2, R, HALF), BF16),
        ),
        in_specs=[hbm] * 3,
        out_specs=(hbm,) * 5 + (vm, hbm),
        scratch_shapes=[
            pltpu.VMEM((2, R, HALF), BF16),
            pltpu.VMEM((SLOTS, CH, 2 * E), BF16),
            pltpu.VMEM((SLOTS, CH, 2 * E), BF16),
            pltpu.VMEM((8 * D, E), BF16),
            pltpu.VMEM((8 * D, E), F32),
            pltpu.VMEM((D, 4 * E), BF16),
            pltpu.VMEM((R, D), BF16),
            pltpu.VMEM((R, E), F32),
            pltpu.VMEM((R, E), BF16),
            pltpu.VMEM((R, E), BF16),
            pltpu.VMEM((2, R, HALF), BF16),
            dma((2, 3, NCH)),
            dma((2, 3, NCH)),
            dma((4, SLOTS)),
            dma((4, SLOTS)),
            dma((5, SLOTS)),
            dma((4,)),
        ],
        compiler_params=pltpu.CompilerParams(
            collective_id=0, has_side_effects=True, vmem_limit_bytes=VMEM_LIMIT
        ),
        cost_estimate=pl.CostEstimate(
            flops=2 * R * D * D, bytes_accessed=16 << 20, transcendentals=R * D
        ),
        name="gather_project",
    )(tokens, cotangent, w)


def attention_kernel(
    q_ref, kv_ref, up_ref, cg_ref, wo_all, all_ids,
    op_ref, gated_ref, dup_ref, dq_ref, dkv_ref, dfar_ref,
    id_ref, idc, acc,
):
    s = lax.axis_index("seq")
    chip = lax.div(s, 2)
    wo_ref = wo_all.at[lax.rem(s, 2)]
    t = pl.program_id(0)

    @pl.when(t == 0)
    def _():
        for b in range(3):
            source = chip - 2 + b
            ids = all_ids[rows_at(jnp.maximum(source, 0) * (R // E), R // E), :]
            ids = jnp.where(source >= 0, ids, -1)
            for j in range(R // E):
                at = b * R + j * E
                row = ids[j : j + 1, :]
                id_ref[0:1, at : at + E] = row
                idc[at : at + E, :] = jnp.broadcast_to(row, (E, E)).T

        @pl.loop(0, WIN // TK)
        def _(j):
            acc[rows_at(j * TK, TK), :] = jnp.zeros((TK, 2 * E), F32)

    def spread(column, width):
        return jnp.concatenate([column] * (width // E), axis=1)

    first = 2 * R // TK
    q = q_ref[...]
    wr = rows_at(2 * R + t * TQ, TQ)
    idq_col = idc[wr, :]
    idq_row = id_ref[0:1, wr]
    start = idq_row[0, 0]
    before = (id_ref[...] < start).astype(jnp.int32)
    low = jnp.sum(before) // TK
    last = first + t * TQ // TK
    uniform = start == idq_row[0, TQ - 1]
    mid = jnp.where(uniform, jnp.minimum(low + 1, last), last)

    def masked(half, ok, kt, causal, row_axis):
        if causal:
            ri = lax.broadcasted_iota(jnp.int32, half.shape, row_axis) + t * TQ
            ci = lax.broadcasted_iota(jnp.int32, half.shape, 1 - row_axis) + (kt - first) * TK
            ok = ok & (ci <= ri)
        return jnp.where(ok, half, OUT_OF_MASK)

    def forward(kt, total, mask=True, causal=False):
        kr = rows_at(kt * TK, TK)
        half = dot(q, kv_ref[kr, E:], NT) * (0.5 * SCALE)
        if mask:
            half = masked(half, spread(idq_col, TK) == id_ref[0:1, kr], kt, causal, 0)
        weights = (half + half * jnp.tanh(half)).astype(BF16)
        return total + dot(weights, kv_ref[kr, :E])

    def backward(kt, total, mask=True, causal=False):
        kr = rows_at(kt * TK, TK)
        k = kv_ref[kr, E:]
        half = dot(k, q, NT) * (0.5 * SCALE)
        if mask:
            half = masked(half, spread(idc[kr, :], TQ) == idq_row, kt, causal, 1)
        tan = jnp.tanh(half)
        weights = half + half * tan
        tan = 0.5 * tan
        slope = (0.5 + tan) + weights * (0.5 - tan)
        ds = (slope * dot(kv_ref[kr, :E], grad, NT)).astype(BF16)
        acc[kr, E:] += dot(ds, q)
        acc[kr, :E] += dot(weights.astype(BF16), grad)
        return total + dot(k.T, ds)

    def over_keys(step, shape=(TQ, E)):
        total = lax.fori_loop(low, mid, step, jnp.zeros(shape, F32))
        total = lax.fori_loop(mid, last, functools.partial(step, mask=False), total)
        for j in range(max(1, TQ // TK)):
            total = step(last + j, total, causal=True)
        return total

    att = over_keys(forward)
    center = att - jnp.mean(att, -1, keepdims=True)
    scale = lax.rsqrt(jnp.mean(center * center, -1, keepdims=True) + FLOOR)
    hn = center * scale
    up = up_ref[...].astype(F32)
    gated = (hn * up).astype(BF16)
    gated_ref[...] = gated
    op_ref[0] = dot(gated, wo_ref[:, :HALF]).astype(BF16)
    op_ref[1] = dot(gated, wo_ref[:, HALF:]).astype(BF16)
    gg = dot(cg_ref[0], wo_ref[:, :HALF], NT) + dot(cg_ref[1], wo_ref[:, HALF:], NT)
    dup_ref[...] = gg * hn
    b = gg * up
    grad = (
        scale * (b - jnp.mean(b, -1, keepdims=True) - hn * jnp.mean(b * hn, -1, keepdims=True))
    ).astype(BF16)
    dq_ref[...] = over_keys(backward, (E, TQ)).T * SCALE

    @pl.when(t == R // TQ - 1)
    def _():
        @pl.loop(0, R // TK)
        def _(j):
            rr = rows_at(j * TK, TK)
            own = rows_at(2 * R + j * TK, TK)
            dkv_ref[rr, :E] = acc[own, :E]
            dkv_ref[rr, E:] = acc[own, E:] * SCALE
            for k in range(2):
                src = rows_at(k * R + j * TK, TK)
                dfar_ref[k, rr, :E] = acc[src, :E].astype(BF16)
                dfar_ref[k, rr, E:] = (acc[src, E:] * SCALE).astype(BF16)


def attention(q, kv, up, cg, wo, ids):
    vm = pl.BlockSpec(memory_space=pltpu.VMEM)
    tile = pl.BlockSpec((TQ, E), lambda t: (t, 0))
    halves = pl.BlockSpec((2, TQ, HALF), lambda t: (0, t, 0))
    return pl.pallas_call(
        attention_kernel,
        grid=(R // TQ,),
        out_shape=(
            jax.ShapeDtypeStruct((2, R, HALF), BF16),
            jax.ShapeDtypeStruct((R, E), BF16),
            jax.ShapeDtypeStruct((R, E), F32),
            jax.ShapeDtypeStruct((R, E), F32),
            jax.ShapeDtypeStruct((R, 2 * E), F32),
            jax.ShapeDtypeStruct((2, R, 2 * E), BF16),
        ),
        in_specs=[tile, vm, tile, halves, vm, vm],
        out_specs=(
            halves,
            tile,
            tile,
            tile,
            pl.BlockSpec((R, 2 * E), lambda t: (0, 0)),
            pl.BlockSpec((2, R, 2 * E), lambda t: (0, 0, 0)),
        ),
        scratch_shapes=[
            pltpu.VMEM((1, WIN), jnp.int32),
            pltpu.VMEM((WIN, E), jnp.int32),
            pltpu.VMEM((WIN, 2 * E), F32),
        ],
        compiler_params=pltpu.CompilerParams(vmem_limit_bytes=VMEM_LIMIT),
        cost_estimate=pl.CostEstimate(
            flops=7 * 2 * R * R * 2 * E, bytes_accessed=16 << 20, transcendentals=4 * R * R
        ),
        name="attention",
    )(q, kv, up, cg, wo, ids)


class Summed:
    def __init__(self, me, rows, grads, bufs, sems, at):
        self.me, self.rows, self.grads, self.bufs = me, rows, grads, bufs
        self.sems, self.at = sems, at
        self.done = []

    def copy(self, src, dst, stage, k, device):
        copy = Copy(src, dst, self.sems, (self.at, stage, k), device).start()
        self.done.append(copy)
        return copy

    def peers(self, here, step):
        s, c = self.me.s, self.me.c
        there = [lax.rem(here + k, 4) for k in (1, 2, 3)]
        return [(v, (s + step * (v - here), c)) for v in there]

    def start(self):
        zbuf, zrecv = self.bufs[0:2]
        n = self.rows // 4
        zbuf[...] = self.grads[...].astype(BF16)
        self.zc = [
            self.copy(zbuf.at[rows_at(v * n, n)], zrecv.at[k], 0, k, device)
            for k, (v, device) in enumerate(self.peers(self.me.z, 8))
        ]

    def over_y(self):
        zrecv, yall = self.bufs[1:3]
        n = self.rows // 4
        for copy in self.zc:
            copy.wait_recv()
        total = self.grads[rows_at(self.me.z * n, n), :]
        for k in range(3):
            total = total + zrecv[k].astype(F32)
        spot = yall.at[self.me.y]
        spot[...] = total.astype(BF16)
        self.yc = [
            self.copy(spot, spot, 1, k, device) for k, (_, device) in enumerate(self.peers(self.me.y, 2))
        ]

    def over_x(self):
        yall, xall = self.bufs[2:4]
        for copy in self.yc:
            copy.wait_recv()
        total = (yall[0].astype(F32) + yall[1].astype(F32)) + (yall[2].astype(F32) + yall[3].astype(F32))
        spot = xall.at[self.me.xl]
        spot[...] = total.astype(BF16)
        self.xc = self.copy(spot, spot, 2, 0, self.me.xpeer)

    def back_z(self):
        xall, whole = self.bufs[3:5]
        me = self.me
        self.xc.wait_recv()
        spot = whole.at[me.core, me.z]
        spot[...] = (xall[0].astype(F32) + xall[1].astype(F32)).astype(BF16)
        self.gz = [
            self.copy(spot, spot, 3, k, device) for k, (_, device) in enumerate(self.peers(me.z, 8))
        ]
        self.gc = [self.copy(spot, spot, 4, 0, me.other)]

    def back_core(self):
        me = self.me
        for k in range(3):
            self.gz[k].wait_recv()
            spot = self.bufs[4].at[me.core, lax.rem(me.z + 3 - k, 4)]
            self.gc.append(self.copy(spot, spot, 4, k + 1, me.other))

    def finish(self):
        for copy in self.gc:
            copy.wait_recv()

    def wait_send(self):
        for copy in self.done:
            copy.wait_send()

    @staticmethod
    def scratch(rows):
        n = rows // 4
        return [
            pltpu.VMEM((rows, 2 * E), BF16),
            pltpu.VMEM((3, n, 2 * E), BF16),
            pltpu.VMEM((4, n, 2 * E), BF16),
            pltpu.VMEM((2, n, 2 * E), BF16),
        ]


EARLY = D + 2 * E
INV_ROOT = 1.0 / 256.0


def gradient_kernel(
    tok_in, cot_in, w_in, nb_in, rs_in, cg_in, gated_in, op_in, dup_in, dq_in, dkv_in, dfar_in,
    out_ref, gt_ref, early_all, late_all,
    tok_ref, cot_ref, w_ref, nb_ref, rs_ref, cg_ref, gated_ref, op_ref, dup_ref, dq_ref, dkv_ref, dfar_ref, ls,
    hopped, back, yvia, nvia, slope, gp, part, chip_sum, to_col, from_col, early_g, late_g, *rest,
):
    early_bufs, late_bufs = rest[:4] + (early_all,), rest[4:8] + (late_all,)
    bss, brs, sss, srs, ass, ars = rest[8:]
    me = Place()
    c, core, chip = me.c, me.core, me.chip
    behind = me.at_chip(chip - 1)
    round_to = me.at_chip(me.in_ring(1))
    source = me.in_ring(-1)
    handed_to = me.at_chip(source - 2)
    two_on = lax.rem(chip + 2, CHIPS)
    two_y = lax.rem(two_on, 4)
    hander = me.at_chip(two_on - two_y + lax.rem(two_y + 1, 4))
    early = Summed(me, EARLY, early_g, early_bufs, (ass, ars), 0)
    late = Summed(me, D, late_g, late_bufs, (ass, ars), 1)
    greet(
        [me.other, me.far, me.at_chip(chip + 1), me.at_chip(chip + 4), round_to, me.at_chip(source)]
        + [hander, me.xpeer]
        + [device for _, device in early.peers(me.y, 2) + early.peers(me.z, 8)],
        14,
    )

    base = core * T
    obase = (1 - core) * T

    order = (
        (nb_in, nb_ref), (w_in, w_ref), (dup_in, dup_ref), (dq_in, dq_ref), (gated_in, gated_ref),
        (cg_in, cg_ref), (op_in.at[:, rows_at(base, T)], op_ref), (dfar_in.at[1], dfar_ref),
        (dkv_in, dkv_ref), (rs_in, rs_ref), (tok_in, tok_ref), (cot_in, cot_ref),
    )
    loads = [pltpu.make_async_copy(src, dst, ls.at[k]) for k, (src, dst) in enumerate(order)]

    def mine_of(kind, half, i):
        if kind == 0:
            return op_ref[half, pl.ds(i * CH, CH)]
        return part[half, rows_at(base + i * CH, CH)]

    def to_core(kind, i):
        src = (op_in, part)[kind].at[:, rows_at(obase + i * CH, CH)]
        dst = chip_sum.at[kind, :, pl.ds(i * CH, CH)]
        return Copy(src, dst, (sss, srs), (kind, 0, i), me.other).start()

    def across(kind, i, copy):
        copy.wait_recv()
        here = pl.ds(i * CH, CH)
        mine = mine_of(kind, 1 - c, i).astype(F32)
        to_col[kind, here] = (mine + chip_sum[kind, 1 - c, here].astype(F32)).astype(BF16)
        return Copy(
            to_col.at[kind, here], from_col.at[kind, here], (sss, srs), (kind, 1, i), me.far
        ).start()

    def finish(kind, i, copy):
        copy.wait_recv()
        here = pl.ds(i * CH, CH)
        own, out = ((tok_ref, out_ref), (cot_ref, gt_ref))[kind]
        total = mine_of(kind, c, i).astype(F32)
        total = total + chip_sum[kind, c, here].astype(F32)
        total = total + from_col[kind, here].astype(F32)
        out[here] = (own[here].astype(F32) + total).astype(BF16)

    near, hop, direct = {}, {}, {}
    for i in range(SLOTS):
        rr = pl.ds(i * CH, CH)
        near[i] = Near(
            me, -1, dfar_in.at[1, rr] if i in AROUND else back.at[2, rr], nvia.at[i], back.at[1, rr],
            (bss, brs), (i,),
        )
        if i in AROUND:
            hop[i] = Copy(
                dfar_in.at[0, rr], yvia.at[i], (bss, brs), (2, i), round_to, chip > 1, source > 1
            )
            direct[i] = Copy(
                yvia.at[i], back.at[0, rr], (bss, brs), (3, i), handed_to, source > 1, chip < CHIPS - 2
            )
        else:
            hop[i] = Copy(
                dfar_in.at[0, rr], hopped.at[i], (bss, brs), (2, i), behind,
                chip > 1, (chip > 0) & (chip < CHIPS - 1),
            )
    joined = [i for i in range(SLOTS) if i not in AROUND]
    for i in joined:
        hop[i].start()
    for i in AROUND:
        hop[i].start()
        near[i].start()
    for copy in loads:
        copy.start()
    out_core = [to_core(0, i) for i in range(NCH)]

    SR = 512
    for copy in loads[:4]:
        copy.wait()

    @pl.loop(0, R // SR)
    def _(i):
        rr = rows_at(i * SR, SR)
        half = 0.5 * dot(nb_ref[rr, :], w_ref[...])
        tan = jnp.tanh(half)
        silu = half + half * tan
        tan = 0.5 * tan
        sl = (0.5 + tan) + silu * (0.5 - tan)
        gp[rr, :E] = (dup_ref[rr, :] * sl[:, :E]).astype(BF16)
        gp[rr, E : 2 * E] = (dq_ref[rr, :] * sl[:, E : 2 * E]).astype(BF16)
        slope[rr, :] = sl[:, 2 * E :]

    for copy in loads[4:6]:
        copy.wait()
    early_g[:D, :] = dot(nb_ref[...], gp[:, : 2 * E], TN)
    for j in range(2):
        early_g[D + j * E : D + (j + 1) * E, :] = dot(gated_ref[...], cg_ref[j], TN)
    early.start()

    for copy in loads[6:]:
        copy.wait()
    out_far = [across(0, i, out_core[i]) for i in range(NCH)]

    for i in joined:
        rr = pl.ds(i * CH, CH)
        back[2, rr] = dfar_ref[rr]

        @pl.when((chip > 0) & (chip < CHIPS - 1))
        def _():
            hop[i].copy.wait_recv()
            back[2, rr] = (dfar_ref[rr].astype(F32) + hopped[i].astype(F32)).astype(BF16)

        near[i].start()
    for i in AROUND:
        hop[i].wait_recv()
        direct[i].start()
    for i in list(AROUND) + joined:
        near[i].hand_on()
    early.over_y()

    for i in list(AROUND) + joined:
        rr = pl.ds(i * CH, CH)
        near[i].wait_recv()

        @pl.when(chip == CHIPS - 1)
        def _():
            back[1, rr] = jnp.zeros((CH, 2 * E), BF16)

        g = dkv_ref[rr, :]
        if i in AROUND:
            direct[i].wait_recv()

            @pl.when(chip >= CHIPS - 2)
            def _():
                back[0, rr] = jnp.zeros((CH, 2 * E), BF16)

            g = g + back[0, rr].astype(F32)
        gp[rr, 2 * E :] = ((g + back[1, rr].astype(F32)) * slope[rr, :]).astype(BF16)

    late_g[...] = dot(nb_ref[...], gp[:, 2 * E :], TN)
    late.start()
    early.over_x()

    def tokens_back(start):
        rr = rows_at(start, CH)
        g = dot(gp[rr, :], w_ref[...], NT)
        nb = nb_ref[rr, :].astype(F32)
        inv = rs_ref[rr, 0:1]
        g = inv * (g - jnp.mean(g, -1, keepdims=True) - nb * jnp.mean(g * nb, -1, keepdims=True))
        part[0, rr] = g[:, :HALF].astype(BF16)
        part[1, rr] = g[:, HALF:].astype(BF16)

    gt_core = []
    for i in range(NCH):
        tokens_back(obase + i * CH)
        gt_core.append(to_core(1, i))
    early.back_z()
    gt_far = []
    for i in range(NCH):
        tokens_back(base + i * CH)
        gt_far.append(across(1, i, gt_core[i]))
    late.over_y()
    for i in range(NCH):
        finish(0, i, out_far[i])
    early.back_core()
    late.over_x()
    late.back_z()
    early.finish()
    late.back_core()
    for i in range(NCH):
        finish(1, i, gt_far[i])
    late.finish()
    for copies in (near, hop, direct):
        for copy in copies.values():
            copy.wait_send()
    for copy in out_core + out_far + gt_core + gt_far + [early, late]:
        copy.wait_send()


def gradients(*operands):
    vm = pl.BlockSpec(memory_space=pltpu.VMEM)
    hbm = pl.BlockSpec(memory_space=pl.ANY)
    dma = pltpu.SemaphoreType.DMA
    loaded = [list(x.shape) for x in operands]
    loaded[7][1] = T
    loaded[11] = [R, 2 * E]
    return pl.pallas_call(
        gradient_kernel,
        out_shape=(
            jax.ShapeDtypeStruct((T, HALF), BF16),
            jax.ShapeDtypeStruct((T, HALF), BF16),
            jax.ShapeDtypeStruct((2, 4, EARLY // 4, 2 * E), BF16),
            jax.ShapeDtypeStruct((2, 4, D // 4, 2 * E), BF16),
        ),
        in_specs=[hbm] * 12,
        out_specs=(vm,) * 4,
        scratch_shapes=[pltpu.VMEM(tuple(d), x.dtype) for d, x in zip(loaded, operands)]
        + [
            dma((12,)),
            pltpu.VMEM((SLOTS, CH, 2 * E), BF16),
            pltpu.VMEM((3, R, 2 * E), BF16),
            pltpu.VMEM((SLOTS, CH, 2 * E), BF16),
            pltpu.VMEM((SLOTS, CH, 2 * E), BF16),
            pltpu.VMEM((R, 2 * E), F32),
            pltpu.VMEM((R, 4 * E), BF16),
            pltpu.VMEM((2, R, HALF), BF16),
            pltpu.VMEM((2, 2, T, HALF), BF16),
            pltpu.VMEM((2, T, HALF), BF16),
            pltpu.VMEM((2, T, HALF), BF16),
            pltpu.VMEM((EARLY, 2 * E), F32),
            pltpu.VMEM((D, 2 * E), F32),
        ]
        + Summed.scratch(EARLY)
        + Summed.scratch(D)
        + [
            dma((4, SLOTS)),
            dma((4, SLOTS)),
            dma((2, 2, NCH)),
            dma((2, 2, NCH)),
            dma((2, 5, 4)),
            dma((2, 5, 4)),
        ],
        compiler_params=pltpu.CompilerParams(
            collective_id=1, has_side_effects=True, vmem_limit_bytes=VMEM_LIMIT
        ),
        cost_estimate=pl.CostEstimate(
            flops=7 * R * D * D, bytes_accessed=16 << 20, transcendentals=R * D
        ),
        name="gradients",
    )(*operands)


def widen_kernel(out_in, gt_in, early_ref, late_ref, out_ref, gt_ref, gwi_ref, gwo_ref, ls):
    passed = [
        pltpu.make_async_copy(src, dst, ls.at[k])
        for k, (src, dst) in enumerate(((out_in, out_ref), (gt_in, gt_ref)))
    ]
    for copy in passed:
        copy.start()
    n = EARLY // 4
    for h in range(2):
        for z in range(4):
            at = 0
            while at < n:
                d = z * n + at
                end = next(b for b in (D, D + E, EARLY) if b > d)
                size = min(n - at, end - d)
                piece = early_ref[h, z, at : at + size, :].astype(F32) * INV_ROOT
                if d < D:
                    for j in range(2):
                        gwi_ref[pl.ds(8 * d + 4 * j + h, size, stride=8), :] = piece[:, j * E : (j + 1) * E]
                else:
                    q, e = divmod(d - D, E)
                    gwo_ref[h, e : e + size, q * HALF : (q + 1) * HALF] = piece
                at += size
            m = D // 4
            piece = late_ref[h, z].astype(F32) * INV_ROOT
            for j in range(2):
                gwi_ref[pl.ds(8 * z * m + 4 * j + 2 + h, m, stride=8), :] = piece[:, j * E : (j + 1) * E]
    for copy in passed:
        copy.wait()


def widen(out, gt, early, late):
    vm = pl.BlockSpec(memory_space=pltpu.VMEM)
    hbm = pl.BlockSpec(memory_space=pl.ANY)
    return pl.pallas_call(
        widen_kernel,
        out_shape=(
            jax.ShapeDtypeStruct((T, HALF), BF16),
            jax.ShapeDtypeStruct((T, HALF), BF16),
            jax.ShapeDtypeStruct((8 * D, E), F32),
            jax.ShapeDtypeStruct((2, E, D), F32),
        ),
        in_specs=[hbm, hbm, vm, vm],
        out_specs=(hbm, hbm, vm, vm),
        scratch_shapes=[pltpu.SemaphoreType.DMA((2,))],
        compiler_params=pltpu.CompilerParams(vmem_limit_bytes=VMEM_LIMIT),
        name="widen",
    )(out, gt, early, late)


def shards(tokens, cotangent, weight_in, weight_out, history_ids):
    w, nb, inv, q, up, kv, cg = project(tokens, cotangent, weight_in.reshape(8 * D, E))
    op, gated, dup, dq, dkv, dfar = attention(
        q, kv.reshape(WIN, 2 * E), up, cg, weight_out, history_ids.reshape(-1, E)
    )
    out, gt, gwi, gwo = widen(
        *gradients(tokens, cotangent, w, nb, inv, cg, gated, op, dup, dq, dkv, dfar)
    )
    return out, gt, gwi.reshape(D, 4, 2, E), gwo


def solution(mesh):
    placed = (
        P("seq", "col"),
        P("seq", "col"),
        P(None, None, "col", None),
        P("col", None, None),
        P(),
    )
    return jax.shard_map(
        shards,
        mesh=mesh,
        in_specs=placed,
        out_specs=(
            P("seq", "col"),
            P("seq", "col"),
            P(None, None, "col", None),
            P("col", None, None),
        ),
        check_vma=False,
    )
```

time: 226 us -> 233 us (1.031)
  Pallas kernels: 219 us -> 231 us
  local copies, waits for them, and re-layouts: 6.08 us -> 0 us
    pallas_call x1 -> x2, Pallas kernels: 27.8 us -> 63.3 us  [the longest x1 35.6 us: widen(): pl.pallas_call(widen_kernel, out_shape=(jax.ShapeDtypeStruct((T, HALF), B...]
    pallas_call x1, Pallas kernels: 135 us -> 120 us  [gradients(): pl.pallas_call(gradient_kernel, out_shape=(jax.ShapeDtypeStruct((T, HALF)...]
    pallas_call x1, Pallas kernels: 56.5 us -> 48.1 us  [project(): pl.pallas_call(project_kernel, out_shape=(jax.ShapeDtypeStruct((D, 4 * E)...]
    unnamed x8 -> x0, local copies, waits for them, and re-layouts: 6.08 us -> none
where the time goes in v3:
time: 233 us; the launch traced here: 232 us
  Pallas kernels  231 us (99%)
    pallas_call x1, Pallas kernels, gradients(): pl.pallas_call(gradient_kernel, out_shape=(jax.ShapeDtypeStruct((T, HALF)...  120 us
    pallas_call x1, Pallas kernels, project(): pl.pallas_call(project_kernel, out_shape=(jax.ShapeDtypeStruct((D, 4 * E)...  48.1 us
    pallas_call x1, Pallas kernels, widen(): pl.pallas_call(widen_kernel, out_shape=(jax.ShapeDtypeStruct((T, HALF), B...  35.6 us
    pallas_call x1, Pallas kernels, attention(): pl.pallas_call(attention_kernel, grid=(R // TQ,), out_shape=(jax.ShapeDty...  27.6 us

profile of v3, /device:TPU:1, one launch (start us, length us, event | category | flops | bytes accessed | tf_op | source)
XLA Modules:
  0.0 232.3 jit_solution(14053211469555382463)
XLA Ops:
  0.6 48.1 %gather_project.1 = (bf16[512,512]{1,0:T(8,128)(2,1)}, bf16[2048,512]{1,0:T(8,128)(2,1)}, f32[2048,128]{1,0:T(8,128)}, bf16[2048,128]{1,0:T(8,128)(2,1)}, bf16[2...) custom-call(bf16[1024,256]{1,0:T(8,128)(2,1)} %tok_in.1, ...), custom_call_target="tpu_custom_call" | custom-call | flops 1073741824 | bytes 16777216 | tf_op jit(solution)/shard_map/gather_project/pallas_call | solution.py:304
  48.7 27.6 %attention.1 = (bf16[2,2048,256]{2,1,0:T(8,128)(2,1)}, bf16[2048,128]{1,0:T(8,128)(2,1)}, f32[2048,128]{1,0:T(8,128)}, f32[2048,128]{1,0:T(8,128)}, f32[2048,256]{1,0:T(8,128)}, /*index=5*/bf16[2,2048,256]{2,1,0:T(8,128)(2,1)}) custom-call(bf16[2048,128]{1,0:T(8,128)(2,1)} %get-tuple-element.29.q_ref, bf16[6144,256]{1,0:T(8,128)(2,1)} %bitcast.7, ...), custom_call_target="tpu_custom_call" | custom-call | flops 15032385536 | bytes 16777216 | tf_op jit(solution)/shard_map/attention/pallas_call | solution.py:459
  76.4 120.0 %gradients.1 = (bf16[1024,256]{1,0:T(8,128)(2,1)}, bf16[1024,256]{1,0:T(8,128)(2,1)}, bf16[2,4,192,256]{3,2,1,0:T(8,128)(2,1)}, bf16[2,4,128,256]{3,2,1,0:T(8,128)(2,1)}) custom-call(bf16[1024,256]{1,0:T(8,128)(2,1)} %tok_in.1, bf16[1024,256]{1,0:T(8,128)(2,1)} %cot_in.1, bf16[512,512]{1,0:T(8,128)(2,1)} %get-tuple-element.25.w_in, ...), custom_call_target="tpu_custom_call" | custom-call | flops 3758096384 | bytes 16777216 | tf_op jit(solution)/shard_map/gradients/pallas_call | solution.py:784
  196.4 35.6 %widen.1 = (bf16[1024,256]{1,0:T(8,128)(2,1)}, bf16[1024,256]{1,0:T(8,128)(2,1)}, f32[4096,128]{1,0:T(8,128)}, f32[2,128,512]{2,1,0:T(8,128)}) custom-call(bf16[1024,256]{1,0:T(8,128)(2,1)} %get-tuple-element.38.out_in, bf16[1024,256]{1,0:T(8,128)(2,1)} %get-tuple-element.39.gt_in, bf16[2,4,192,256]{3,2,1,0:T(8,128)(2,1)} %get-tuple-element.40.early_ref, ...), custom_call_target="tpu_custom_call" | custom-call | tf_op jit(solution)/shard_map/widen/pallas_call | solution.py:864

commit v4 on v3

--- a/solution.py
+++ b/solution.py
@@ -827,13 +827,9 @@
     )(*operands)
 
 
-def widen_kernel(out_in, gt_in, early_ref, late_ref, out_ref, gt_ref, gwi_ref, gwo_ref, ls):
-    passed = [
-        pltpu.make_async_copy(src, dst, ls.at[k])
-        for k, (src, dst) in enumerate(((out_in, out_ref), (gt_in, gt_ref)))
-    ]
-    for copy in passed:
-        copy.start()
+def widen_kernel(out_in, gt_in, early_ref, late_ref, out_ref, gt_ref, gwi_ref, gwo_ref):
+    out_ref[...] = out_in[...]
+    gt_ref[...] = gt_in[...]
     n = EARLY // 4
     for h in range(2):
         for z in range(4):
@@ -854,13 +850,10 @@
             piece = late_ref[h, z].astype(F32) * INV_ROOT
             for j in range(2):
                 gwi_ref[pl.ds(8 * z * m + 4 * j + 2 + h, m, stride=8), :] = piece[:, j * E : (j + 1) * E]
-    for copy in passed:
-        copy.wait()
 
 
 def widen(out, gt, early, late):
     vm = pl.BlockSpec(memory_space=pltpu.VMEM)
-    hbm = pl.BlockSpec(memory_space=pl.ANY)
     return pl.pallas_call(
         widen_kernel,
         out_shape=(
@@ -869,9 +862,8 @@
             jax.ShapeDtypeStruct((8 * D, E), F32),
             jax.ShapeDtypeStruct((2, E, D), F32),
         ),
-        in_specs=[hbm, hbm, vm, vm],
-        out_specs=(hbm, hbm, vm, vm),
-        scratch_shapes=[pltpu.SemaphoreType.DMA((2,))],
+        in_specs=[vm] * 4,
+        out_specs=(vm,) * 4,
         compiler_params=pltpu.CompilerParams(vmem_limit_bytes=VMEM_LIMIT),
         name="widen",
     )(out, gt, early, late)

time: 233 us -> 203 us (0.87)
  Pallas kernels: 231 us -> 202 us
    pallas_call x1, Pallas kernels: 35.6 us -> 3.72 us  [widen(): pl.pallas_call(widen_kernel, out_shape=(jax.ShapeDtypeStruct((T, HALF), B...]
    pallas_call x1, Pallas kernels: 120 us -> 122 us  [gradients(): pl.pallas_call(gradient_kernel, out_shape=(jax.ShapeDtypeStruct((T, HALF)...]
where the time goes in v4:
time: 203 us
  Pallas kernels  202 us (100%)
    pallas_call x1, Pallas kernels, gradients(): pl.pallas_call(gradient_kernel, out_shape=(jax.ShapeDtypeStruct((T, HALF)...  122 us
    pallas_call x1, Pallas kernels, project(): pl.pallas_call(project_kernel, out_shape=(jax.ShapeDtypeStruct((D, 4 * E)...  48.1 us
    pallas_call x1, Pallas kernels, attention(): pl.pallas_call(attention_kernel, grid=(R // TQ,), out_shape=(jax.ShapeDty...  27.6 us

profile of v4, /device:TPU:1, one launch (start us, length us, event | category | flops | bytes accessed | tf_op | source)
XLA Modules:
  0.0 202.6 jit_solution(5974401080945827445)
XLA Ops:
  0.6 48.1 %gather_project.1 = (bf16[512,512]{1,0:T(8,128)(2,1)}, bf16[2048,512]{1,0:T(8,128)(2,1)}, f32[2048,128]{1,0:T(8,128)}, bf16[2048,128]{1,0:T(8,128)(2,1)}, bf16[2...) custom-call(bf16[1024,256]{1,0:T(8,128)(2,1)} %tok_in.1, ...), custom_call_target="tpu_custom_call" | custom-call | flops 1073741824 | bytes 16777216 | tf_op jit(solution)/shard_map/gather_project/pallas_call | solution.py:304
  48.7 27.6 %attention.1 = (bf16[2,2048,256]{2,1,0:T(8,128)(2,1)}, bf16[2048,128]{1,0:T(8,128)(2,1)}, f32[2048,128]{1,0:T(8,128)}, f32[2048,128]{1,0:T(8,128)}, f32[2048,256]{1,0:T(8,128)}, /*index=5*/bf16[2,2048,256]{2,1,0:T(8,128)(2,1)}) custom-call(bf16[2048,128]{1,0:T(8,128)(2,1)} %get-tuple-element.29.q_ref, bf16[6144,256]{1,0:T(8,128)(2,1)} %bitcast.7, ...), custom_call_target="tpu_custom_call" | custom-call | flops 15032385536 | bytes 16777216 | tf_op jit(solution)/shard_map/attention/pallas_call | solution.py:459
  76.4 122.5 %gradients.1 = (bf16[1024,256]{1,0:T(8,128)(2,1)}, bf16[1024,256]{1,0:T(8,128)(2,1)}, bf16[2,4,192,256]{3,2,1,0:T(8,128)(2,1)}, bf16[2,4,128,256]{3,2,1,0:T(8,128)(2,1)}) custom-call(bf16[1024,256]{1,0:T(8,128)(2,1)} %tok_in.1, bf16[1024,256]{1,0:T(8,128)(2,1)} %cot_in.1, bf16[512,512]{1,0:T(8,128)(2,1)} %get-tuple-element.25.w_in, ...), custom_call_target="tpu_custom_call" | custom-call | flops 3758096384 | bytes 16777216 | tf_op jit(solution)/shard_map/gradients/pallas_call | solution.py:784
  198.9 3.7 %widen.1 = (bf16[1024,256]{1,0:T(8,128)(2,1)}, bf16[1024,256]{1,0:T(8,128)(2,1)}, f32[4096,128]{1,0:T(8,128)}, f32[2,128,512]{2,1,0:T(8,128)}) custom-call(bf16[1024,256]{1,0:T(8,128)(2,1)} %get-tuple-element.38.out_in, bf16[1024,256]{1,0:T(8,128)(2,1)} %get-tuple-element.39.gt_in, bf16[2,4,192,256]{3,2,1,0:T(8,128)(2,1)} %get-tuple-element.40.early_ref, ...), custom_call_target="tpu_custom_call" | custom-call | tf_op jit(solution)/shard_map/widen/pallas_call | solution.py:857

commit v5 on v4

--- a/solution.py
+++ b/solution.py
@@ -28,6 +28,7 @@
 OUT_OF_MASK = -32.0
 SLOTS = R // CH
 AROUND = (2, 3, 5, 6, 7)
+BACK_AROUND = (4, 5, 6, 7, 0)
 CHIPS = 32
 VMEM_LIMIT = 56 * 1024 * 1024
 
@@ -346,7 +347,7 @@
 def attention_kernel(
     q_ref, kv_ref, up_ref, cg_ref, wo_all, all_ids,
     op_ref, gated_ref, dup_ref, dq_ref, dkv_ref, dfar_ref,
-    id_ref, idc, acc,
+    id_ref, idc, acc, tot, tot_t,
 ):
     s = lax.axis_index("seq")
     chip = lax.div(s, 2)
@@ -391,15 +392,15 @@
             ok = ok & (ci <= ri)
         return jnp.where(ok, half, OUT_OF_MASK)
 
-    def forward(kt, total, mask=True, causal=False):
+    def forward(kt, mask=True, causal=False):
         kr = rows_at(kt * TK, TK)
         half = dot(q, kv_ref[kr, E:], NT) * (0.5 * SCALE)
         if mask:
             half = masked(half, spread(idq_col, TK) == id_ref[0:1, kr], kt, causal, 0)
         weights = (half + half * jnp.tanh(half)).astype(BF16)
-        return total + dot(weights, kv_ref[kr, :E])
-
-    def backward(kt, total, mask=True, causal=False):
+        tot[...] += dot(weights, kv_ref[kr, :E])
+
+    def backward(kt, mask=True, causal=False):
         kr = rows_at(kt * TK, TK)
         k = kv_ref[kr, E:]
         half = dot(k, q, NT) * (0.5 * SCALE)
@@ -412,16 +413,24 @@
         ds = (slope * dot(kv_ref[kr, :E], grad, NT)).astype(BF16)
         acc[kr, E:] += dot(ds, q)
         acc[kr, :E] += dot(weights.astype(BF16), grad)
-        return total + dot(k.T, ds)
-
-    def over_keys(step, shape=(TQ, E)):
-        total = lax.fori_loop(low, mid, step, jnp.zeros(shape, F32))
-        total = lax.fori_loop(mid, last, functools.partial(step, mask=False), total)
+        tot_t[...] += dot(k.T, ds)
+
+    def over_keys(step, total):
+        total[...] = jnp.zeros_like(total)
+
+        @pl.loop(low, mid)
+        def _(kt):
+            step(kt)
+
+        @pl.loop(mid, last)
+        def _(kt):
+            step(kt, mask=False)
+
         for j in range(max(1, TQ // TK)):
-            total = step(last + j, total, causal=True)
-        return total
-
-    att = over_keys(forward)
+            step(last + j, causal=True)
+        return total[...]
+
+    att = over_keys(forward, tot)
     center = att - jnp.mean(att, -1, keepdims=True)
     scale = lax.rsqrt(jnp.mean(center * center, -1, keepdims=True) + FLOOR)
     hn = center * scale
@@ -436,7 +445,7 @@
     grad = (
         scale * (b - jnp.mean(b, -1, keepdims=True) - hn * jnp.mean(b * hn, -1, keepdims=True))
     ).astype(BF16)
-    dq_ref[...] = over_keys(backward, (E, TQ)).T * SCALE
+    dq_ref[...] = over_keys(backward, tot_t).T * SCALE
 
     @pl.when(t == R // TQ - 1)
     def _():
@@ -480,6 +489,8 @@
             pltpu.VMEM((1, WIN), jnp.int32),
             pltpu.VMEM((WIN, E), jnp.int32),
             pltpu.VMEM((WIN, 2 * E), F32),
+            pltpu.VMEM((TQ, E), F32),
+            pltpu.VMEM((E, TQ), F32),
         ],
         compiler_params=pltpu.CompilerParams(vmem_limit_bytes=VMEM_LIMIT),
         cost_estimate=pl.CostEstimate(
@@ -642,14 +653,17 @@
         total = total + from_col[kind, here].astype(F32)
         out[here] = (own[here].astype(F32) + total).astype(BF16)
 
+    def slot_rows(i):
+        return rows_at((base if i < NCH else obase) + i % NCH * CH, CH)
+
     near, hop, direct = {}, {}, {}
     for i in range(SLOTS):
-        rr = pl.ds(i * CH, CH)
+        rr = slot_rows(i)
         near[i] = Near(
-            me, -1, dfar_in.at[1, rr] if i in AROUND else back.at[2, rr], nvia.at[i], back.at[1, rr],
+            me, -1, dfar_in.at[1, rr] if i in BACK_AROUND else back.at[2, rr], nvia.at[i], back.at[1, rr],
             (bss, brs), (i,),
         )
-        if i in AROUND:
+        if i in BACK_AROUND:
             hop[i] = Copy(
                 dfar_in.at[0, rr], yvia.at[i], (bss, brs), (2, i), round_to, chip > 1, source > 1
             )
@@ -661,10 +675,10 @@
                 dfar_in.at[0, rr], hopped.at[i], (bss, brs), (2, i), behind,
                 chip > 1, (chip > 0) & (chip < CHIPS - 1),
             )
-    joined = [i for i in range(SLOTS) if i not in AROUND]
+    joined = [i for i in range(SLOTS) if i not in BACK_AROUND]
     for i in joined:
         hop[i].start()
-    for i in AROUND:
+    for i in BACK_AROUND:
         hop[i].start()
         near[i].start()
     for copy in loads:
@@ -699,7 +713,7 @@
     out_far = [across(0, i, out_core[i]) for i in range(NCH)]
 
     for i in joined:
-        rr = pl.ds(i * CH, CH)
+        rr = slot_rows(i)
         back[2, rr] = dfar_ref[rr]
 
         @pl.when((chip > 0) & (chip < CHIPS - 1))
@@ -708,15 +722,17 @@
             back[2, rr] = (dfar_ref[rr].astype(F32) + hopped[i].astype(F32)).astype(BF16)
 
         near[i].start()
-    for i in AROUND:
+    for i in BACK_AROUND:
         hop[i].wait_recv()
         direct[i].start()
-    for i in list(AROUND) + joined:
+    for i in list(BACK_AROUND) + joined:
         near[i].hand_on()
     early.over_y()
 
-    for i in list(AROUND) + joined:
-        rr = pl.ds(i * CH, CH)
+    gt_core = {}
+    gt_far = []
+    for turn, i in enumerate(list(BACK_AROUND) + joined):
+        rr = slot_rows(i)
         near[i].wait_recv()
 
         @pl.when(chip == CHIPS - 1)
@@ -724,7 +740,7 @@
             back[1, rr] = jnp.zeros((CH, 2 * E), BF16)
 
         g = dkv_ref[rr, :]
-        if i in AROUND:
+        if i in BACK_AROUND:
             direct[i].wait_recv()
 
             @pl.when(chip >= CHIPS - 2)
@@ -732,30 +748,29 @@
                 back[0, rr] = jnp.zeros((CH, 2 * E), BF16)
 
             g = g + back[0, rr].astype(F32)
-        gp[rr, 2 * E :] = ((g + back[1, rr].astype(F32)) * slope[rr, :]).astype(BF16)
-
-    late_g[...] = dot(nb_ref[...], gp[:, 2 * E :], TN)
-    late.start()
-    early.over_x()
-
-    def tokens_back(start):
-        rr = rows_at(start, CH)
+        g = ((g + back[1, rr].astype(F32)) * slope[rr, :]).astype(BF16)
+        gp[rr, 2 * E :] = g
+        nb = nb_ref[rr, :]
+        if turn == 0:
+            late_g[...] = dot(nb, g, TN)
+        else:
+            late_g[...] += dot(nb, g, TN)
+        if turn == SLOTS - 1:
+            late.start()
         g = dot(gp[rr, :], w_ref[...], NT)
-        nb = nb_ref[rr, :].astype(F32)
+        nb = nb.astype(F32)
         inv = rs_ref[rr, 0:1]
         g = inv * (g - jnp.mean(g, -1, keepdims=True) - nb * jnp.mean(g * nb, -1, keepdims=True))
         part[0, rr] = g[:, :HALF].astype(BF16)
         part[1, rr] = g[:, HALF:].astype(BF16)
-
-    gt_core = []
-    for i in range(NCH):
-        tokens_back(obase + i * CH)
-        gt_core.append(to_core(1, i))
-    early.back_z()
-    gt_far = []
-    for i in range(NCH):
-        tokens_back(base + i * CH)
-        gt_far.append(across(1, i, gt_core[i]))
+        if i >= NCH:
+            gt_core[i - NCH] = to_core(1, i - NCH)
+        else:
+            gt_far.append(across(1, i, gt_core[i]))
+        if turn == 3:
+            early.over_x()
+        if turn == 6:
+            early.back_z()
     late.over_y()
     for i in range(NCH):
         finish(0, i, out_far[i])
@@ -770,7 +785,7 @@
     for copies in (near, hop, direct):
         for copy in copies.values():
             copy.wait_send()
-    for copy in out_core + out_far + gt_core + gt_far + [early, late]:
+    for copy in out_core + out_far + list(gt_core.values()) + gt_far + [early, late]:
         copy.wait_send()
 
 

time: 203 us -> 205 us (level)
    pallas_call x1, Pallas kernels: 122 us -> 125 us  [gradients(): pl.pallas_call(gradient_kernel, out_shape=(jax.ShapeDtypeStruct((T, HALF)...]
where the time goes in v5:
time: 205 us; the launch traced here: 204 us
  Pallas kernels  204 us (100%)
    pallas_call x1, Pallas kernels, gradients(): pl.pallas_call(gradient_kernel, out_shape=(jax.ShapeDtypeStruct((T, HALF)...  125 us
    pallas_call x1, Pallas kernels, project(): pl.pallas_call(project_kernel, out_shape=(jax.ShapeDtypeStruct((D, 4 * E)...  48.1 us
    pallas_call x1, Pallas kernels, attention(): pl.pallas_call(attention_kernel, grid=(R // TQ,), out_shape=(jax.ShapeDty...  27.1 us

profile of v5, /device:TPU:1, one launch (start us, length us, event | category | flops | bytes accessed | tf_op | source)
XLA Modules:
  0.0 204.5 jit_solution(8392466990318255000)
XLA Ops:
  0.6 48.1 %gather_project.1 = (bf16[512,512]{1,0:T(8,128)(2,1)}, bf16[2048,512]{1,0:T(8,128)(2,1)}, f32[2048,128]{1,0:T(8,128)}, bf16[2048,128]{1,0:T(8,128)(2,1)}, bf16[2...) custom-call(bf16[1024,256]{1,0:T(8,128)(2,1)} %tok_in.1, ...), custom_call_target="tpu_custom_call" | custom-call | flops 1073741824 | bytes 16777216 | tf_op jit(solution)/shard_map/gather_project/pallas_call | solution.py:305
  48.7 27.1 %attention.1 = (bf16[2,2048,256]{2,1,0:T(8,128)(2,1)}, bf16[2048,128]{1,0:T(8,128)(2,1)}, f32[2048,128]{1,0:T(8,128)}, f32[2048,128]{1,0:T(8,128)}, f32[2048,256]{1,0:T(8,128)}, /*index=5*/bf16[2,2048,256]{2,1,0:T(8,128)(2,1)}) custom-call(bf16[2048,128]{1,0:T(8,128)(2,1)} %get-tuple-element.29.q_ref, bf16[6144,256]{1,0:T(8,128)(2,1)} %bitcast.7, ...), custom_call_target="tpu_custom_call" | custom-call | flops 15032385536 | bytes 16777216 | tf_op jit(solution)/shard_map/attention/pallas_call | solution.py:468
  75.8 124.9 %gradients.1 = (bf16[1024,256]{1,0:T(8,128)(2,1)}, bf16[1024,256]{1,0:T(8,128)(2,1)}, bf16[2,4,192,256]{3,2,1,0:T(8,128)(2,1)}, bf16[2,4,128,256]{3,2,1,0:T(8,128)(2,1)}) custom-call(bf16[1024,256]{1,0:T(8,128)(2,1)} %tok_in.1, bf16[1024,256]{1,0:T(8,128)(2,1)} %cot_in.1, bf16[512,512]{1,0:T(8,128)(2,1)} %get-tuple-element.25.w_in, ...), custom_call_target="tpu_custom_call" | custom-call | flops 3758096384 | bytes 16777216 | tf_op jit(solution)/shard_map/gradients/pallas_call | solution.py:799
  200.7 3.7 %widen.1 = (bf16[1024,256]{1,0:T(8,128)(2,1)}, bf16[1024,256]{1,0:T(8,128)(2,1)}, f32[4096,128]{1,0:T(8,128)}, f32[2,128,512]{2,1,0:T(8,128)}) custom-call(bf16[1024,256]{1,0:T(8,128)(2,1)} %get-tuple-element.38.out_in, bf16[1024,256]{1,0:T(8,128)(2,1)} %get-tuple-element.39.gt_in, bf16[2,4,192,256]{3,2,1,0:T(8,128)(2,1)} %get-tuple-element.40.early_ref, ...), custom_call_target="tpu_custom_call" | custom-call | tf_op jit(solution)/shard_map/widen/pallas_call | solution.py:872

commit v6 on v5

--- a/solution.py
+++ b/solution.py
@@ -27,7 +27,7 @@
 SCALE = E**-0.5
 OUT_OF_MASK = -32.0
 SLOTS = R // CH
-AROUND = (2, 3, 5, 6, 7)
+AROUND = (0, 1, 2, 4, 5)
 BACK_AROUND = (4, 5, 6, 7, 0)
 CHIPS = 32
 VMEM_LIMIT = 56 * 1024 * 1024
@@ -102,18 +102,23 @@
 
 
 class Near:
-    def __init__(self, me, step, src, via, dst, sems, at):
+    def __init__(self, me, step, src, via, dst, sems, at, x_last):
         edge = 3 if step > 0 else 0
         first, last = (0, CHIPS - 1) if step > 0 else (CHIPS - 1, 0)
         cross = me.y == edge
         goes = me.chip != last
         self.comes = me.chip != first
         self.straight = Copy(src, dst, sems, (0,) + at, me.at_chip(me.chip + step), goes & ~cross, self.comes)
-        beyond = me.chip > 3 if step > 0 else me.chip < CHIPS - 4
-        self.aside = Copy(
-            src, via, sems, (1,) + at, me.at_chip(me.chip + 4 * step), goes & cross, beyond & cross
-        )
-        self.onward = Copy(via, dst, sems, (0,) + at, me.at_chip(me.in_ring(step)), beyond & cross)
+        relay = me.chip + 4 * step
+        target = me.in_ring(step)
+        hands_on = cross & (me.chip > 3 if step > 0 else me.chip < CHIPS - 4)
+        if x_last:
+            before = 15 if step > 0 else 16
+            relay = jnp.where(me.chip == before, first, relay)
+            hands_on = (hands_on & (me.chip != before + 4 * step)) | (me.chip == first)
+            target = jnp.where(me.chip == first, before + step, target)
+        self.aside = Copy(src, via, sems, (1,) + at, me.at_chip(relay), goes & cross, hands_on)
+        self.onward = Copy(via, dst, sems, (0,) + at, me.at_chip(target), hands_on)
 
     def start(self):
         self.straight.start()
@@ -133,8 +138,8 @@
 
 def project_kernel(
     tok_ref, cot_ref, w_ref,
-    wh_ref, nb_ref, rs_ref, q_ref, up_ref, kv_ref, cg_ref,
-    xg, yvia, nvia, wv, wf, wh, nb, inv_all, qv, upv, cg, oss, ors, kss, krs, ls, lcg,
+    wt_ref, nb_ref, rs_ref, q_ref, up_ref, kv_ref, cg_ref, nt_ref, sl_ref,
+    xg, yvia, nvia, wv, wf, wh, nb, inv_all, qv, upv, cg, wt, nt, sl, oss, ors, kss, krs, ls, lcg,
 ):
     me = Place()
     c, core, chip = me.c, me.core, me.chip
@@ -146,8 +151,9 @@
     two_y = lax.rem(two_back, 4)
     hander = me.at_chip(two_back - two_y + lax.rem(two_y + 3, 4))
     greet(
-        [me.other, me.far, me.at_chip(chip - 1), me.at_chip(chip - 4), round_to, me.at_chip(source), hander],
-        7,
+        [me.other, me.far, me.at_chip(chip - 1), me.at_chip(chip - 4), round_to, me.at_chip(source), hander]
+        + [me.at_chip(chip + 15), me.xpeer],
+        9,
     )
 
     base = core * T
@@ -198,13 +204,11 @@
         first = wf[pl.ds(2 * part, D, stride=8), :]
         second = wf[pl.ds(2 * part + 1, D, stride=8), :]
         wh[:, lanes] = jnp.where(core == 0, first, second).astype(BF16)
-    store(4, 0, wh, wh_ref)
-
     near, hop, direct, chained = {}, {}, {}, {}
     for slot in range(SLOTS):
         rr = rows_at((base if slot < NCH else obase) + slot % NCH * CH, CH)
         mine = kv_ref.at[2, rr]
-        near[slot] = Near(me, 1, mine, nvia.at[slot], kv_ref.at[1, rr], (kss, krs), (slot,))
+        near[slot] = Near(me, 1, mine, nvia.at[slot], kv_ref.at[1, rr], (kss, krs), (slot,), slot % 2 == 0)
         if slot in AROUND:
             hop[slot] = Copy(
                 mine, yvia.at[slot], (kss, krs), (2, slot), round_to,
@@ -239,6 +243,7 @@
         near[slot].start()
         if slot in AROUND:
             hop[slot].start()
+        sl[rr] = half
         nb[rr, :HALF] = n0
         nb[rr, HALF:] = n1
         inv_all[rr] = jnp.broadcast_to(inv, (CH, E))
@@ -262,20 +267,32 @@
         o_copies[0, i].wait_recv()
         f_copies[0, i].wait_recv()
         compute(NCH + i)
+        if i == 2:
+            for j in range(NCH):
+                x_copies[1, j].start()
+                o_copies[1, j].start()
         if i:
             for slot in (i - 1, NCH + i - 1):
                 near[slot].hand_on()
                 if slot in AROUND:
                     hand_on(slot)
-    for i in range(NCH):
-        x_copies[1, i].start()
-        o_copies[1, i].start()
     for slot in (NCH - 1, SLOTS - 1):
         near[slot].hand_on()
-        if slot in AROUND:
-            hand_on(slot)
-    for slot in (0, NCH, 1):
+    late = (NCH - 1, SLOTS - 1)
+    for slot in [i for i in range(SLOTS) if i not in AROUND] + [i for i in late if i in AROUND]:
         hand_on(slot)
+    wt[...] = wh[...].T
+    store(4, 0, wt, wt_ref)
+    for i in range(SLOTS):
+        rr = pl.ds(i * CH, CH)
+        half = sl[rr]
+        tan = jnp.tanh(half)
+        silu = half + half * tan
+        tan = 0.5 * tan
+        sl[rr] = (0.5 + tan) + silu * (0.5 - tan)
+        store(5, i, sl.at[rr], sl_ref.at[rr])
+        nt[:, i * CH : (i + 1) * CH] = nb[rr].T
+    store(4, 1, nt, nt_ref)
     for i in range(NCH):
         x_copies[1, i].wait_recv()
         f_copies[1, i].start()
@@ -312,9 +329,11 @@
             jax.ShapeDtypeStruct((R, E), BF16),
             jax.ShapeDtypeStruct((3, R, 2 * E), BF16),
             jax.ShapeDtypeStruct((2, R, HALF), BF16),
+            jax.ShapeDtypeStruct((D, R), BF16),
+            jax.ShapeDtypeStruct((R, 4 * E), F32),
         ),
         in_specs=[hbm] * 3,
-        out_specs=(hbm,) * 5 + (vm, hbm),
+        out_specs=(hbm,) * 5 + (vm,) + (hbm,) * 3,
         scratch_shapes=[
             pltpu.VMEM((2, R, HALF), BF16),
             pltpu.VMEM((SLOTS, CH, 2 * E), BF16),
@@ -327,11 +346,14 @@
             pltpu.VMEM((R, E), BF16),
             pltpu.VMEM((R, E), BF16),
             pltpu.VMEM((2, R, HALF), BF16),
+            pltpu.VMEM((4 * E, D), BF16),
+            pltpu.VMEM((D, R), BF16),
+            pltpu.VMEM((R, 4 * E), F32),
             dma((2, 3, NCH)),
             dma((2, 3, NCH)),
             dma((4, SLOTS)),
             dma((4, SLOTS)),
-            dma((5, SLOTS)),
+            dma((6, SLOTS)),
             dma((4,)),
         ],
         compiler_params=pltpu.CompilerParams(
@@ -590,10 +612,10 @@
 
 
 def gradient_kernel(
-    tok_in, cot_in, w_in, nb_in, rs_in, cg_in, gated_in, op_in, dup_in, dq_in, dkv_in, dfar_in,
+    tok_in, cot_in, w_in, nb_in, rs_in, cg_in, gated_in, op_in, dup_in, dq_in, dkv_in, dfar_in, nt_in, sl_in,
     out_ref, gt_ref, early_all, late_all,
-    tok_ref, cot_ref, w_ref, nb_ref, rs_ref, cg_ref, gated_ref, op_ref, dup_ref, dq_ref, dkv_ref, dfar_ref, ls,
-    hopped, back, yvia, nvia, slope, gp, part, chip_sum, to_col, from_col, early_g, late_g, *rest,
+    tok_ref, cot_ref, w_ref, nb_ref, rs_ref, cg_ref, gated_ref, op_ref, dup_ref, dq_ref, dkv_ref, dfar_ref, nt_ref, slope, ls,
+    hopped, back, yvia, nvia, gp, part, chip_sum, to_col, from_col, early_g, late_g, *rest,
 ):
     early_bufs, late_bufs = rest[:4] + (early_all,), rest[4:8] + (late_all,)
     bss, brs, sss, srs, ass, ars = rest[8:]
@@ -610,18 +632,18 @@
     late = Summed(me, D, late_g, late_bufs, (ass, ars), 1)
     greet(
         [me.other, me.far, me.at_chip(chip + 1), me.at_chip(chip + 4), round_to, me.at_chip(source)]
-        + [hander, me.xpeer]
+        + [hander, me.xpeer, me.at_chip(chip - 15)]
         + [device for _, device in early.peers(me.y, 2) + early.peers(me.z, 8)],
-        14,
+        15,
     )
 
     base = core * T
     obase = (1 - core) * T
 
     order = (
-        (nb_in, nb_ref), (w_in, w_ref), (dup_in, dup_ref), (dq_in, dq_ref), (gated_in, gated_ref),
+        (sl_in, slope), (dup_in, dup_ref), (dq_in, dq_ref), (nt_in, nt_ref), (gated_in, gated_ref),
         (cg_in, cg_ref), (op_in.at[:, rows_at(base, T)], op_ref), (dfar_in.at[1], dfar_ref),
-        (dkv_in, dkv_ref), (rs_in, rs_ref), (tok_in, tok_ref), (cot_in, cot_ref),
+        (dkv_in, dkv_ref), (nb_in, nb_ref), (w_in, w_ref), (rs_in, rs_ref), (tok_in, tok_ref), (cot_in, cot_ref),
     )
     loads = [pltpu.make_async_copy(src, dst, ls.at[k]) for k, (src, dst) in enumerate(order)]
 
@@ -661,7 +683,7 @@
         rr = slot_rows(i)
         near[i] = Near(
             me, -1, dfar_in.at[1, rr] if i in BACK_AROUND else back.at[2, rr], nvia.at[i], back.at[1, rr],
-            (bss, brs), (i,),
+            (bss, brs), (i,), i % 2 == 0,
         )
         if i in BACK_AROUND:
             hop[i] = Copy(
@@ -686,24 +708,18 @@
     out_core = [to_core(0, i) for i in range(NCH)]
 
     SR = 512
-    for copy in loads[:4]:
+    for copy in loads[:3]:
         copy.wait()
 
     @pl.loop(0, R // SR)
     def _(i):
         rr = rows_at(i * SR, SR)
-        half = 0.5 * dot(nb_ref[rr, :], w_ref[...])
-        tan = jnp.tanh(half)
-        silu = half + half * tan
-        tan = 0.5 * tan
-        sl = (0.5 + tan) + silu * (0.5 - tan)
-        gp[rr, :E] = (dup_ref[rr, :] * sl[:, :E]).astype(BF16)
-        gp[rr, E : 2 * E] = (dq_ref[rr, :] * sl[:, E : 2 * E]).astype(BF16)
-        slope[rr, :] = sl[:, 2 * E :]
-
-    for copy in loads[4:6]:
+        gp[rr, :E] = (dup_ref[rr, :] * slope[rr, :E]).astype(BF16)
+        gp[rr, E : 2 * E] = (dq_ref[rr, :] * slope[rr, E : 2 * E]).astype(BF16)
+
+    for copy in loads[3:6]:
         copy.wait()
-    early_g[:D, :] = dot(nb_ref[...], gp[:, : 2 * E], TN)
+    early_g[:D, :] = dot(nt_ref[...], gp[:, : 2 * E])
     for j in range(2):
         early_g[D + j * E : D + (j + 1) * E, :] = dot(gated_ref[...], cg_ref[j], TN)
     early.start()
@@ -748,17 +764,17 @@
                 back[0, rr] = jnp.zeros((CH, 2 * E), BF16)
 
             g = g + back[0, rr].astype(F32)
-        g = ((g + back[1, rr].astype(F32)) * slope[rr, :]).astype(BF16)
+        g = ((g + back[1, rr].astype(F32)) * slope[rr, 2 * E :]).astype(BF16)
         gp[rr, 2 * E :] = g
-        nb = nb_ref[rr, :]
+        tokens_of = nt_ref[:, rr]
         if turn == 0:
-            late_g[...] = dot(nb, g, TN)
+            late_g[...] = dot(tokens_of, g)
         else:
-            late_g[...] += dot(nb, g, TN)
+            late_g[...] += dot(tokens_of, g)
         if turn == SLOTS - 1:
             late.start()
-        g = dot(gp[rr, :], w_ref[...], NT)
-        nb = nb.astype(F32)
+        g = dot(gp[rr, :], w_ref[...])
+        nb = nb_ref[rr, :].astype(F32)
         inv = rs_ref[rr, 0:1]
         g = inv * (g - jnp.mean(g, -1, keepdims=True) - nb * jnp.mean(g * nb, -1, keepdims=True))
         part[0, rr] = g[:, :HALF].astype(BF16)
@@ -804,16 +820,15 @@
             jax.ShapeDtypeStruct((2, 4, EARLY // 4, 2 * E), BF16),
             jax.ShapeDtypeStruct((2, 4, D // 4, 2 * E), BF16),
         ),
-        in_specs=[hbm] * 12,
+        in_specs=[hbm] * 14,
         out_specs=(vm,) * 4,
         scratch_shapes=[pltpu.VMEM(tuple(d), x.dtype) for d, x in zip(loaded, operands)]
         + [
-            dma((12,)),
+            dma((14,)),
             pltpu.VMEM((SLOTS, CH, 2 * E), BF16),
             pltpu.VMEM((3, R, 2 * E), BF16),
             pltpu.VMEM((SLOTS, CH, 2 * E), BF16),
             pltpu.VMEM((SLOTS, CH, 2 * E), BF16),
-            pltpu.VMEM((R, 2 * E), F32),
             pltpu.VMEM((R, 4 * E), BF16),
             pltpu.VMEM((2, R, HALF), BF16),
             pltpu.VMEM((2, 2, T, HALF), BF16),
@@ -885,12 +900,14 @@
 
 
 def shards(tokens, cotangent, weight_in, weight_out, history_ids):
-    w, nb, inv, q, up, kv, cg = project(tokens, cotangent, weight_in.reshape(8 * D, E))
+    wt, nb, inv, q, up, kv, cg, nt, slope = project(tokens, cotangent, weight_in.reshape(8 * D, E))
     op, gated, dup, dq, dkv, dfar = attention(
         q, kv.reshape(WIN, 2 * E), up, cg, weight_out, history_ids.reshape(-1, E)
     )
     out, gt, gwi, gwo = widen(
-        *gradients(tokens, cotangent, w, nb, inv, cg, gated, op, dup, dq, dkv, dfar)
+        *gradients(
+            tokens, cotangent, wt, nb, inv, cg, gated, op, dup, dq, dkv, dfar, nt, slope
+        )
     )
     return out, gt, gwi.reshape(D, 4, 2, E), gwo
 

time: 205 us -> 189 us (0.922)
  Pallas kernels: 204 us -> 188 us
    pallas_call x1, Pallas kernels: 125 us -> 112 us  [gradients(): pl.pallas_call(gradient_kernel, out_shape=(jax.ShapeDtypeStruct((T, HALF)...]
where the time goes in v6:
time: 189 us
  Pallas kernels  188 us (99%)
    pallas_call x1, Pallas kernels, gradients(): pl.pallas_call(gradient_kernel, out_shape=(jax.ShapeDtypeStruct((T, HALF)...  112 us
    pallas_call x1, Pallas kernels, project(): pl.pallas_call(project_kernel, out_shape=(jax.ShapeDtypeStruct((D, 4 * E)...  46.1 us
    pallas_call x1, Pallas kernels, attention(): pl.pallas_call(attention_kernel, grid=(R // TQ,), out_shape=(jax.ShapeDty...  27.1 us

profile of v6, /device:TPU:1, one launch (start us, length us, event | category | flops | bytes accessed | tf_op | source)
XLA Modules:
  0.0 189.1 jit_solution(4718189282833266815)
XLA Ops:
  0.6 46.1 %gather_project.1 = (bf16[512,512]{1,0:T(8,128)(2,1)}, bf16[2048,512]{1,0:T(8,128)(2,1)}, f32[2048,128]{1,0:T(8,128)}, bf16[2048,128]{1,0:T(8,128)(2,1)}, bf16[2...) custom-call(bf16[1024,256]{1,0:T(8,128)(2,1)} %tok_in.1, ...), custom_call_target="tpu_custom_call" | custom-call | flops 1073741824 | bytes 16777216 | tf_op jit(solution)/shard_map/gather_project/pallas_call | solution.py:322
  46.7 27.1 %attention.1 = (bf16[2,2048,256]{2,1,0:T(8,128)(2,1)}, bf16[2048,128]{1,0:T(8,128)(2,1)}, f32[2048,128]{1,0:T(8,128)}, f32[2048,128]{1,0:T(8,128)}, f32[2048,256]{1,0:T(8,128)}, /*index=5*/bf16[2,2048,256]{2,1,0:T(8,128)(2,1)}) custom-call(bf16[2048,128]{1,0:T(8,128)(2,1)} %get-tuple-element.31.q_ref, bf16[6144,256]{1,0:T(8,128)(2,1)} %bitcast.7, ...), custom_call_target="tpu_custom_call" | custom-call | flops 15032385536 | bytes 16777216 | tf_op jit(solution)/shard_map/attention/pallas_call | solution.py:490
  73.8 111.6 %gradients.1 = (bf16[1024,256]{1,0:T(8,128)(2,1)}, bf16[1024,256]{1,0:T(8,128)(2,1)}, bf16[2,4,192,256]{3,2,1,0:T(8,128)(2,1)}, bf16[2,4,128,256]{3,2,1,0:T(8,128)(2,1)}) custom-call(bf16[1024,256]{1,0:T(8,128)(2,1)} %tok_in.1, bf16[1024,256]{1,0:T(8,128)(2,1)} %cot_in.1, bf16[512,512]{1,0:T(8,128)(2,1)} %get-tuple-element.27.w_in, ...), custom_call_target="tpu_custom_call" | custom-call | flops 3758096384 | bytes 16777216 | tf_op jit(solution)/shard_map/gradients/pallas_call | solution.py:815
  185.4 3.7 %widen.1 = (bf16[1024,256]{1,0:T(8,128)(2,1)}, bf16[1024,256]{1,0:T(8,128)(2,1)}, f32[4096,128]{1,0:T(8,128)}, f32[2,128,512]{2,1,0:T(8,128)}) custom-call(bf16[1024,256]{1,0:T(8,128)(2,1)} %get-tuple-element.42.out_in, bf16[1024,256]{1,0:T(8,128)(2,1)} %get-tuple-element.43.gt_in, bf16[2,4,192,256]{3,2,1,0:T(8,128)(2,1)} %get-tuple-element.44.early_ref, ...), custom_call_target="tpu_custom_call" | custom-call | tf_op jit(solution)/shard_map/widen/pallas_call | solution.py:887
